TPU v7x, 512 devices: a whole 4x4x16 slice. The times are simulated.
512 devices in a mesh: tm: 16 (over z), height: 32 (over x, y, core).
Axes of the slice: x: 4, y: 4, z: 16, core: 2. Of those that a mesh axis runs over, the one named last changes fastest.
Arguments:
- latent: bfloat16 [32, 64, 16, 256], P('tm', 'height'), may hold values from -6 to 6
- target_frames: bfloat16 [32, 128, 32, 128], P('tm', 'height'), may hold values from -6 to 6
- master: float32 [256, 3456], P('height'), may hold values from -1.5 to 1.5
- first_moment: float32 [256, 3456], P('height'), may hold values from -18 to 18
- second_moment: float32 [256, 3456], P('height'), may hold values from 1 to 10
- ema_weights: float32 [256, 3456], P('height'), may hold values from -6 to 6
Outputs:
- new_master: float32 [256, 3456], P('height')
- new_first: float32 [256, 3456], P('height')
- new_second: float32 [256, 3456], P('height')
- new_ema: float32 [256, 3456], P('height')
- latent_grad: bfloat16 [32, 64, 16, 256], P('tm', 'height')
- recon_loss: float32 [], replicated
All inputs are finite; a program needn't handle non-finite values.
Results may differ from a plain program's by a relative error of at most 0.0056.
Values may be sent and summed in bfloat16 or wider, within the bound.
A program may use at most 64 MiB of HBM per device.

v0:
```python
import math

import jax
import jax.numpy as jnp
from jax import lax
from jax.sharding import PartitionSpec as P

learn_rate = 0.3
beta_first = 0.9
beta_second = 0.99
ema_decay = 0.9
adam_eps = 1e-08


def passed_along(array, axis, by):
    size = lax.axis_size(axis)
    pairs = [(i, i + by) for i in range(size) if 0 <= i + by < size]
    return lax.ppermute(array, axis, pairs)


def with_halo(array, sides, width):
    for axis, dim in sides:
        size, length = (lax.axis_size(axis), array.shape[dim])
        up = [(i, (i + 1) % size) for i in range(size - 1)]
        down = [(j, i) for i, j in up]
        last = lax.slice_in_dim(array, length - width, length, axis=dim)
        first = lax.slice_in_dim(array, 0, width, axis=dim)
        before = lax.ppermute(last, axis, up)
        after = lax.ppermute(first, axis, down)
        array = jnp.concatenate([before, array, after], axis=dim)
    return array


def tap_offsets():
    return [
        (tap_time, tap_row, tap_col)
        for tap_time in range(3)
        for tap_row in range(3)
        for tap_col in range(3)
    ]


def per_device(latent, target_frames, master, first_moment, second_moment, ema_weights):
    frames, low_rows, low_cols, channels = latent.shape
    outputs = target_frames.shape[3]
    rows = 2 * low_rows
    cols = 2 * low_cols
    cells = frames * rows * cols
    scale = 1.0 / math.sqrt(27 * channels)
    kernel_shard = (master * scale).astype(jnp.bfloat16)
    earlier = passed_along(latent, "tm", 1)
    joined = jnp.concatenate([earlier, latent], axis=0)
    rimmed = with_halo(joined, (("height", 1),), 1)
    upsampled = jnp.repeat(jnp.repeat(rimmed, 2, axis=1), 2, axis=2)[:, 1 : rows + 3]
    padded = jnp.pad(upsampled, ((0, 0), (0, 0), (1, 1), (0, 0)))
    inputs_tap = [
        padded[
            tap_time : tap_time + frames, tap_row : tap_row + rows, tap_col : tap_col + cols
        ].reshape(cells, channels)
        for tap_time, tap_row, tap_col in tap_offsets()
    ]
    empty = jnp.zeros((cells, outputs), jnp.float32)
    total = empty
    weight_piece = lax.all_gather(kernel_shard, "height", axis=0, tiled=True)
    for index in range(27):
        window = inputs_tap[index]
        total = total + jnp.dot(
            window,
            weight_piece[:, index * outputs : (index + 1) * outputs],
            preferred_element_type=jnp.float32,
        )
    result = total
    misfit = result - target_frames.reshape(cells, outputs).astype(jnp.float32)
    squared = lax.psum(jnp.sum(misfit * misfit), ("tm", "height"))
    recon_loss = squared / (cells * outputs * lax.axis_size("tm") * lax.axis_size("height"))
    out_grad = misfit.astype(jnp.bfloat16)
    grad_block = out_grad.reshape(frames, rows, cols, outputs)
    later = passed_along(grad_block, "tm", -1)
    grad_joined = jnp.concatenate([grad_block, later], axis=0)
    grad_rimmed = with_halo(grad_joined, (("height", 1),), 1)
    grad_padded = jnp.pad(grad_rimmed, ((0, 0), (0, 0), (1, 1), (0, 0)))
    grads_tap = [
        grad_padded[
            2 - tap_time : 2 - tap_time + frames,
            2 - tap_row : 2 - tap_row + rows,
            2 - tap_col : 2 - tap_col + cols,
        ].reshape(cells, outputs)
        for tap_time, tap_row, tap_col in tap_offsets()
    ]
    weight_piece = lax.all_gather(kernel_shard, "height", axis=0, tiled=True)
    row_count = weight_piece.shape[0]
    total = jnp.zeros((cells, row_count), jnp.float32)
    for index in range(27):
        column = weight_piece[:, index * outputs : (index + 1) * outputs]
        total = total + lax.dot_general(
            grads_tap[index], column, (((1,), (1,)), ((), ())), preferred_element_type=jnp.float32
        )
    spread = total.reshape(frames, rows, cols, row_count)
    latent_grad = (
        spread.reshape(frames, low_rows, 2, low_cols, 2, channels)
        .sum(axis=(2, 4))
        .astype(jnp.bfloat16)
    )
    pieces = []
    for index in range(27):
        window = inputs_tap[index]
        pieces.append(
            lax.dot_general(
                window, out_grad, (((0,), (0,)), ((), ())), preferred_element_type=jnp.float32
            )
        )
    whole_grad = lax.psum(jnp.concatenate(pieces, axis=1), "tm")
    grad_shard = lax.psum_scatter(whole_grad, "height", scatter_dimension=0, tiled=True)
    kernel_grad = scale * grad_shard
    new_first = beta_first * first_moment + (1.0 - beta_first) * kernel_grad
    new_second = beta_second * second_moment + (1.0 - beta_second) * kernel_grad * kernel_grad
    new_master = master - learn_rate * new_first / (jnp.sqrt(new_second) + adam_eps)
    new_ema = ema_decay * ema_weights + (1.0 - ema_decay) * new_master
    return (new_master, new_first, new_second, new_ema, latent_grad, recon_loss)


def solution(mesh):
    placed = (
        P("tm", "height", None, None),
        P("tm", "height", None, None),
        P("height", None),
        P("height", None),
        P("height", None),
        P("height", None),
    )
    return jax.shard_map(
        per_device,
        mesh=mesh,
        in_specs=placed,
        out_specs=(
            P("height", None),
            P("height", None),
            P("height", None),
            P("height", None),
            P("tm", "height", None, None),
            P(),
        ),
        check_vma=False,
    )
```

profile of v0, /device:TPU:2, one launch (start us, length us, event | category | flops | bytes accessed | tf_op | source)
XLA Modules:
  0.0 398.8 jit_solution(13880081977059874163)
XLA Ops:
  7.2 1.5 multiply_convert_fusion
  8.8 3.8 collective-permute-start
  12.6 1.9 collective-permute-done
  15.3 1.9 collective-permute-start.1
  17.2 5.8 %collective-permute-start.2 = (bf16[4,1,16,256]{3,2,1,0:T(8,128)(2,1)S(1)}, bf16[4,1,16,256]{3,2,1,0:T(8,128)(2,1)S(1)}, u32[]{:S(2)}, u32[]{:S(2)}) collective-permute-start(bf16[4,1,16,256]{3,2,1,0:T(8,128)(2,1)S(1)} %get-tuple-element.74), channel_id=1, source_target_pairs={{1,0},{2,1},{3,2},{4,3},{5,4},{6,5},{7,6},{8,7},{9,8},{10,9},{11,1... | collective-permute-start | bytes 98312 | tf_op jit(solution)/shard_map/ppermute | solution.py:29
  23.0 1.3 dynamic-slice
  25.7 1.4 pad_slice_fusion
  27.3 47.3 %all-gather.2.cloned.1.call-done = bf16[256,3456]{1,0:T(8,128)(2,1)} async-done(((bf16[8,3456]{1,0:T(8,128)(2,1)}), bf16[256,3456]{1,0:T(8,128)(2,1)}) %all-gather.2.cloned.1.call-update) | async-done | bytes 1769488 | tf_op jit(solution)/shard_map/all_gather | solution.py:64
  74.6 1.2 fusion.63
  75.8 1.0 convolution_add_fusion.49
  76.9 1.1 convolution_add_fusion.48
  78.0 1.1 convolution_add_fusion.47
  79.1 1.0 convolution_add_fusion.46
  84.9 0.9 convolution_dynamic-update-slice_fusion.26
  85.8 1.3 collective-permute-start.3
  90.5 0.9 convolution_dynamic-update-slice_fusion.21
  94.0 0.9 convolution_dynamic-update-slice_fusion.17
  99.2 0.9 convolution_dynamic-update-slice_fusion.11
  101.9 0.9 convolution_dynamic-update-slice_fusion.8
  105.3 0.9 convolution_dynamic-update-slice_fusion.4
  107.9 0.9 convolution_dynamic-update-slice_fusion.1
  109.7 106.1 %psum.15 = f32[]{:T(128)} all-reduce(f32[]{:T(128)} %get-tuple-element.67), channel_id=1, replica_groups=mesh['tm'=16,'height'=32] {'tm','height'}, use_global_device_ids=true, to_apply=%region_4.5 | all-reduce | flops 1 | bytes 8 | tf_op jit(solution)/shard_map/psum | solution.py:74
  216.5 1.9 collective-permute-start.4
  218.4 5.8 %collective-permute-start.5 = (bf16[4,1,32,128]{3,2,1,0:T(8,128)(2,1)S(1)}, bf16[4,1,32,128]{3,2,1,0:T(8,128)(2,1)S(1)}, u32[]{:S(2)}, u32[]{:S(2)}) collective-permute-start(bf16[4,1,32,128]{3,2,1,0:T(8,128)(2,1)S(1)} %get-tuple-element.72), channel_id=1, source_target_pairs={{1,0},{2,1},{3,2},{4,3},{5,4},{6,5},{7,6},{8,7},{9,8},{10,9},{11,1... | collective-permute-start | bytes 98312 | tf_op jit(solution)/shard_map/ppermute | solution.py:29
  224.2 1.5 collective-permute-done.5
  231.6 0.9 convolution_add_fusion.1
  232.4 19.0 %all-reduce.8.cloned.1.call-done = f32[256,3456]{0,1:T(8,128)} async-done(((f32[256,3456]{0,1:T(8,128)}), f32[256,3456]{0,1:T(8,128)}) %all-reduce.8.cloned.1.call-update) | async-done | bytes 3538960
  251.5 2.0 constant_dynamic-slice_fusion
  253.5 1.2 copy.25
  254.6 1.2 convolution_add_fusion
  256.8 132.5 %all-reduce.6.cloned.1.call-done = f32[8,3456]{1,0:T(8,128)} async-done(((f32[8,3456]{1,0:T(8,128)}), f32[8,3456]{1,0:T(8,128)}) %all-reduce.6.cloned.1.call-update) | async-done | bytes 110608 | tf_op jit(solution)/shard_map/psum | solution.py:112
  389.3 1.9 multiply_add_fusion
  (130 shorter events, 30.1 us)
Async XLA Ops:
  7.2 67.4 %all-gather.2.cloned.1.call-start = ((), (), s32[]{:S(2)}) async-start(), calls=%async_computation | async-start | bytes 1824768 | tf_op jit(solution)/shard_map/all_gather | solution.py:64
  8.8 242.7 %all-reduce.8.cloned.1.call-start = ((), (), s32[]{:S(2)}) async-start(), calls=%async_computation.2 | async-start | bytes 7077888
  8.8 5.7 %collective-permute-start = (bf16[2,2,16,256]{3,2,1,0:T(8,128)(2,1)}, bf16[2,2,16,256]{3,2,1,0:T(8,128)(2,1)S(1)}, u32[]{:S(2)}, u32[]{:S(2)}) collective-permute-start(bf16[2,2,16,256]{3,2,1,0:T(8,128)(2,1)} %param.6), channel_id=1, source_target_pairs={{0,32},{32,64},{64,96},{96,128},{128,160},{160,192},{192,224},{224... | collective-permute-start | bytes 98312 | tf_op jit(solution)/shard_map/ppermute | solution.py:18
  15.3 9.6 %collective-permute-start.1 = (bf16[4,1,16,256]{3,2,1,0:T(8,128)(2,1)S(1)}, bf16[4,1,16,256]{3,2,1,0:T(8,128)(2,1)S(1)}, u32[]{:S(2)}, u32[]{:S(2)}) collective-permute-start(bf16[4,1,16,256]{3,2,1,0:T(8,128)(2,1)S(1)} %get-tuple-element.73), channel_id=1, source_target_pairs={{0,1},{1,2},{2,3},{3,4},{4,5},{5,6},{6,7},{7,8},{8,9},{9,10},{10,1... | collective-permute-start | bytes 98312 | tf_op jit(solution)/shard_map/ppermute | solution.py:28
  17.2 7.7 %collective-permute-start.2 = (bf16[4,1,16,256]{3,2,1,0:T(8,128)(2,1)S(1)}, bf16[4,1,16,256]{3,2,1,0:T(8,128)(2,1)S(1)}, u32[]{:S(2)}, u32[]{:S(2)}) collective-permute-start(bf16[4,1,16,256]{3,2,1,0:T(8,128)(2,1)S(1)} %get-tuple-element.74), channel_id=1, source_target_pairs={{1,0},{2,1},{3,2},{4,3},{5,4},{6,5},{7,6},{8,7},{9,8},{10,9},{11,1... | collective-permute-start | bytes 98312 | tf_op jit(solution)/shard_map/ppermute | solution.py:29
  27.1 55.9 %copy-start.1 = (bf16[2,4,32,256]{3,2,1,0:T(8,128)(2,1)}, bf16[2,4,32,256]{3,2,1,0:T(8,128)(2,1)S(1)}, u32[]{:S(2)}) copy-start(bf16[2,4,32,256]{3,2,1,0:T(8,128)(2,1)S(1)} %get-tuple-element.38) | copy-start | bytes 393220
  74.6 5.6 %copy-start = (bf16[256,3456]{1,0:T(8,128)(2,1)S(1)}, bf16[256,3456]{1,0:T(8,128)(2,1)}, u32[]{:S(2)}) copy-start(bf16[256,3456]{1,0:T(8,128)(2,1)} %all-gather.2.cloned.1.call-done) | copy-start | bytes 5308420
  74.6 5.6 %copy-start.12 = (bf16[2,4,32,256]{3,2,1,0:T(8,128)(2,1)S(1)}, bf16[2,4,32,256]{3,2,1,0:T(8,128)(2,1)}, u32[]{:S(2)}) copy-start(bf16[2,4,32,256]{3,2,1,0:T(8,128)(2,1)} %get-tuple-element.28) | copy-start | bytes 393220
  74.6 5.8 %copy-start.11 = (bf16[2,4,32,256]{3,2,1,0:T(8,128)(2,1)S(1)}, bf16[2,4,32,256]{3,2,1,0:T(8,128)(2,1)}, u32[]{:S(2)}) copy-start(bf16[2,4,32,256]{3,2,1,0:T(8,128)(2,1)} %get-tuple-element.29) | copy-start | bytes 393220
  74.6 6.2 %copy-start.10 = (bf16[2,4,32,256]{3,2,1,0:T(8,128)(2,1)S(1)}, bf16[2,4,32,256]{3,2,1,0:T(8,128)(2,1)}, u32[]{:S(2)}) copy-start(bf16[2,4,32,256]{3,2,1,0:T(8,128)(2,1)} %get-tuple-element.30) | copy-start | bytes 393220
  75.8 5.1 %copy-start.9 = (bf16[2,4,32,256]{3,2,1,0:T(8,128)(2,1)S(1)}, bf16[2,4,32,256]{3,2,1,0:T(8,128)(2,1)}, u32[]{:S(2)}) copy-start(bf16[2,4,32,256]{3,2,1,0:T(8,128)(2,1)} %get-tuple-element.31) | copy-start | bytes 393220
  78.0 3.4 copy-start.8
  79.1 2.4 copy-start.7
  80.4 1.5 copy-start.6
  80.6 1.5 copy-start.5
  80.9 1.5 copy-start.4
  81.1 1.5 copy-start.3
  82.6 1.5 copy-start.16
  82.6 1.5 copy-start.17
  82.8 2.1 copy-start.15
  83.2 4.8 %copy-start.14 = (bf16[2,4,32,256]{3,2,1,0:T(8,128)(2,1)S(1)}, bf16[2,4,32,256]{3,2,1,0:T(8,128)(2,1)}, u32[]{:S(2)}) copy-start(bf16[2,4,32,256]{3,2,1,0:T(8,128)(2,1)} %get-tuple-element.26) | copy-start | bytes 393220
  83.2 5.6 %copy-start.13 = (bf16[2,4,32,256]{3,2,1,0:T(8,128)(2,1)S(1)}, bf16[2,4,32,256]{3,2,1,0:T(8,128)(2,1)}, u32[]{:S(2)}) copy-start(bf16[2,4,32,256]{3,2,1,0:T(8,128)(2,1)} %get-tuple-element.27) | copy-start | bytes 393220
  85.8 130.7 %collective-permute-start.3 = (bf16[2,4,32,128]{3,2,1,0:T(8,128)(2,1)S(1)}, bf16[2,4,32,128]{3,2,1,0:T(8,128)(2,1)S(1)}, u32[]{:S(2)}, u32[]{:S(2)}) collective-permute-start(bf16[2,4,32,128]{3,2,1,0:T(8,128)(2,1)S(1)} %bitcast.168), channel_id=1, source_target_pairs={{32,0},{64,32},{96,64},{128,96},{160,128},{192,160},{224,192},{256... | collective-permute-start | bytes 196616 | tf_op jit(solution)/shard_map/ppermute | solution.py:18
  94.0 9.6 %copy-start.2 = (bf16[2,4,32,256]{3,2,1,0:T(8,128)(2,1)S(1)}, bf16[2,4,32,256]{3,2,1,0:T(8,128)(2,1)}, u32[]{:S(2)}) copy-start(bf16[2,4,32,256]{3,2,1,0:T(8,128)(2,1)} %copy-done.1) | copy-start | bytes 393220
  109.7 279.6 %all-reduce.6.cloned.1.call-start = ((), (), s32[]{:S(2)}) async-start(), calls=%async_computation.1 | async-start | bytes 221184 | tf_op jit(solution)/shard_map/psum | solution.py:112
  216.5 7.7 %collective-permute-start.4 = (bf16[4,1,32,128]{3,2,1,0:T(8,128)(2,1)S(1)}, bf16[4,1,32,128]{3,2,1,0:T(8,128)(2,1)S(1)}, u32[]{:S(2)}, u32[]{:S(2)}) collective-permute-start(bf16[4,1,32,128]{3,2,1,0:T(8,128)(2,1)S(1)} %get-tuple-element.71), channel_id=1, source_target_pairs={{0,1},{1,2},{2,3},{3,4},{4,5},{5,6},{6,7},{7,8},{8,9},{9,10},{10,1... | collective-permute-start | bytes 98312 | tf_op jit(solution)/shard_map/ppermute | solution.py:28
  218.4 7.3 %collective-permute-start.5 = (bf16[4,1,32,128]{3,2,1,0:T(8,128)(2,1)S(1)}, bf16[4,1,32,128]{3,2,1,0:T(8,128)(2,1)S(1)}, u32[]{:S(2)}, u32[]{:S(2)}) collective-permute-start(bf16[4,1,32,128]{3,2,1,0:T(8,128)(2,1)S(1)} %get-tuple-element.72), channel_id=1, source_target_pairs={{1,0},{2,1},{3,2},{4,3},{5,4},{6,5},{7,6},{8,7},{9,8},{10,9},{11,1... | collective-permute-start | bytes 98312 | tf_op jit(solution)/shard_map/ppermute | solution.py:29
Sparse Core Ops, SparseCore 0:
  11.7 62.8 all-gather.1
  109.8 141.6 all-reduce.7
  254.8 134.4 all-reduce.5
where the time goes:
time: 399 us
  waiting for transfers between devices  202 us (51%)
  blocking collectives  106 us (27%)
  matrix products  40 us (10%)
  starting transfers between devices  20.6 us (5%)
  between operations  17 us (4%)
  local copies, waits for them, and re-layouts  8.5 us (2%)
  other arithmetic  4.4 us (1%)
    psum x1, waiting for transfers between devices, per_device(): whole_grad = lax.psum(jnp.concatenate(pieces, axis=1), 'tm')  132 us
    psum x1, blocking collectives, per_device(): squared = lax.psum(jnp.sum(misfit * misfit), ('tm', 'height'))  106 us
    all_gather x1, waiting for transfers between devices, per_device(): weight_piece = lax.all_gather(kernel_shard, 'height', axis=0, tiled=True)  47.3 us
    dot_general x27, matrix products, per_device(): lax.dot_general(window, out_grad, (((0,), (0,)), ((), ())), preferred_ele...  23.5 us
    unnamed x4, waiting for transfers between devices  19.1 us
    ppermute x2, starting transfers between devices, with_halo(): after = lax.ppermute(first, axis, down)  11.5 us
    dot_general x27, matrix products, per_device(): jnp.dot(window, weight_piece[:, index * outputs:(index + 1) * outputs], p...  9.84 us
  transfers between devices with their start and end apart: 9, of which 5 were waited for; matrix products, arithmetic and copies ran while one was open for 9% of the time, Pallas kernels for 0%

commit v1 on v0

v1 whole, which is shorter than its diff:
```python
import math

import jax
import jax.numpy as jnp
from jax import lax
from jax.experimental import pallas as pl
from jax.experimental.pallas import tpu as pltpu
from jax.sharding import PartitionSpec as P

learn_rate = 0.3
beta_first = 0.9
beta_second = 0.99
ema_decay = 0.9
adam_eps = 1e-08

MESH = pl.DeviceIdType.MESH
F32 = jnp.float32
BF16 = jnp.bfloat16
SCALE = 1.0 / math.sqrt(27 * 256)
WIDE = 640
CUT = 384
PARTS = ((0, CUT), (CUT, WIDE - CUT))
Z = 16


def low_lanes(shape):
    return lax.broadcasted_iota(jnp.int32, shape, len(shape) - 1) < 64


def swap_lanes(v):
    return pltpu.roll(v, 64, axis=v.ndim - 1)


def col_of(shape):
    return lax.broadcasted_iota(jnp.int32, shape, 0) % 16


def from_left(v):
    return jnp.where(col_of(v.shape) == 0, 0.0, pltpu.roll(v, 1, axis=0))


def from_right(v):
    return jnp.where(col_of(v.shape) == 15, 0.0, pltpu.roll(v, v.shape[0] - 1, axis=0))


def split_halves(m):
    low = low_lanes((8, 128))
    zero = jnp.zeros((8, 128), F32)
    halves = ([], [])
    for a in range(3):
        blocks = ([], [])
        for k in range(5):
            t = 9 * a + 2 * k
            even = m[:, t * 128 : (t + 1) * 128]
            odd = m[:, (t + 1) * 128 : (t + 2) * 128] if k < 4 else zero
            blocks[0].append(jnp.where(low, even, swap_lanes(odd)))
            blocks[1].append(jnp.where(low, swap_lanes(even), odd))
        for c in range(2):
            halves[c].append(jnp.concatenate(blocks[c], axis=1))
    return halves


def slot_of(blocks, s):
    return swap_lanes(blocks[s // 2]) if s % 2 else blocks[s // 2]


def outputs_of(z):
    u = []
    for b in range(3):
        z0, z1, z2 = (slot_of(z, 3 * b + e) for e in range(3))
        u.append((from_left(z0) + z1 + z2, z0 + z1 + from_right(z2)))
    out = ([], [])
    for j in range(2):
        common = u[0][j][0:80] + u[2][j][16:96]
        out[0].append(common + u[1][j][16:96])
        out[1].append(common + u[1][j][0:80])
    return out


def folded(g):
    slots = []
    for b in range(3):
        v = []
        for j in range(2):
            g0, g1 = g[0][j], g[1][j]
            v.append((g1[16:80] + g0[16:80], g0[0:64] + g1[16:80], g1[0:64] + g0[0:64])[b])
        slots += [v[1] + from_right(v[0]), v[0] + v[1], from_left(v[1]) + v[0]]
    low = low_lanes((64, 128))
    blocks = []
    for k in range(5):
        odd = swap_lanes(slots[2 * k + 1]) if k < 4 else jnp.zeros((64, 128), F32)
        blocks.append(jnp.where(low, slots[2 * k], odd))
    return blocks


def adam(g, master, first, second, ema):
    new_first = beta_first * first + (1.0 - beta_first) * g
    new_second = beta_second * second + (1.0 - beta_second) * g * g
    new_master = master - learn_rate * new_first / (jnp.sqrt(new_second) + adam_eps)
    new_ema = ema_decay * ema + (1.0 - ema_decay) * new_master
    return new_master, new_first, new_second, new_ema


def remote(src, dst, send_sem, recv_sem, device):
    return pltpu.make_async_remote_copy(
        src_ref=src,
        dst_ref=dst,
        send_sem=send_sem,
        recv_sem=recv_sem,
        device_id=device,
        device_id_type=MESH,
    )


def kernel(
    latent,
    target,
    master,
    first_hbm,
    second_hbm,
    ema_hbm,
    out_master,
    out_first,
    out_second,
    out_ema,
    out_latent,
    out_loss,
    pair_out,
    pair_in,
    weights,
    xe,
    xc,
    te,
    tf,
    tp,
    zs,
    hs,
    dw,
    far_b,
    near_b,
    far_a,
    near_a,
    total,
    zsend_buf,
    zrecv_buf,
    gsend_buf,
    grecv_buf,
    lat_own,
    lat_out,
    lat_in,
    first,
    second,
    ema,
    pair_sem,
    ag_send,
    ag_recv,
    x_send,
    x_recv,
    t_send,
    t_recv,
    rs_send,
    rs_recv,
    z_send,
    z_recv,
    g_send,
    g_recv,
    lat_sem,
    load_sem,
):
    z = lax.axis_index("tm")
    h = lax.axis_index("height")
    c = h % 2
    u = h // 2
    other = 1 - c
    sa, sb = 4 - 3 * c, 1 + 3 * c
    pa = jnp.where(c == 0, u // 4, u % 4)
    pb = jnp.where(c == 0, u % 4, u // 4)

    def unit(da, db):
        return ((pa + da + 4) % 4) * sa + ((pb + db + 4) % 4) * sb

    def dev(chip, core, dz=0):
        return ((z + dz + Z) % Z, chip * 2 + core)

    def hop_a(step):
        return dev(unit(step, 0), c)

    def hop_b(step):
        return dev(unit(0, step), c)

    sibling = dev(u, other)
    above, below = (u + 15) % 16, (u + 1) % 16

    barrier = pltpu.get_barrier_semaphore()
    peers = [hop_a(1), hop_a(-1), hop_b(1), hop_b(-1)]
    for dz in (-1, 0, 1):
        for chip in (above, below):
            for core in range(2):
                peers.append(dev(chip, core, dz))
    for peer in peers:
        pl.semaphore_signal(barrier, inc=1, device_id=peer, device_id_type=MESH)

    def greet(i, carry):
        pl.semaphore_signal(
            barrier, inc=1, device_id=dev(u, (c + i % 2) % 2, i // 2), device_id_type=MESH
        )
        return carry

    lax.fori_loop(1, 2 * Z, greet, 0)

    loads = [
        pltpu.make_async_copy(src, dst, load_sem.at[i])
        for i, (src, dst) in enumerate(((first_hbm, first), (second_hbm, second), (ema_hbm, ema)))
    ]
    for load in loads:
        load.start()

    halves = split_halves(master[...] * SCALE)
    for a in range(3):
        pair_out[a] = jnp.where(c == 0, halves[1][a], halves[0][a])

    pl.semaphore_wait(barrier, len(peers) + 2 * Z - 1)

    sent = []

    def send(*args):
        copy = remote(*args)
        copy.start()
        sent.append(copy)

    def arrived(dst, sem):
        remote(dst, dst, ag_send.at[0], sem, sibling).wait_recv()

    send(pair_out, pair_in, pair_sem.at[0], pair_sem.at[1], sibling)

    own_rows = pl.ds(1 + 2 * c, 2)
    edge = pl.ds(c, 1)
    edge_to = jnp.where(c == 0, above, below)
    edge_row = pl.ds(5 - 5 * c, 1)
    n = 0
    for t, dz in ((0, 1), (1, 0), (2, -1)):
        frames = pl.ds(2 * t, 2)
        for flip in range(2):
            if t == 1 and flip == 0:
                continue
            send(
                latent,
                xe.at[frames, own_rows],
                x_send.at[n],
                x_recv.at[2 * t + c],
                dev(u, (c + flip) % 2, dz),
            )
            n += 1
    for t, dz in ((0, 1), (1, 0), (2, -1)):
        frames = pl.ds(2 * t, 2)
        for core in range(2):
            send(
                latent.at[:, edge],
                xe.at[frames, edge_row],
                x_send.at[n],
                x_recv.at[6 + 2 * t + c],
                dev(edge_to, core, dz),
            )
            n += 1

    arrived(pair_in, pair_sem.at[1])
    for a in range(3):
        mine = jnp.where(c == 0, halves[0][a], halves[1][a])
        theirs = pair_in[a]
        rows = jnp.concatenate(
            [jnp.where(c == 0, mine, theirs), jnp.where(c == 0, theirs, mine)], axis=0
        )
        weights[a, u] = rows.astype(BF16)

    def piece(ref, index, part):
        first_col, width = PARTS[part]
        return ref.at[:, index, :, pl.ds(first_col, width)]

    def spread_unit(hop, index, sem):
        for d, step in enumerate((1, -1)):
            place = weights.at[:, index]
            send(place, place, ag_send.at[sem + d], ag_recv.at[sem + d], hop(step))

    def pass_on(hop, index, sem, d):
        place = piece(weights, index, d)
        send(place, place, ag_send.at[sem + 2 + d], ag_recv.at[sem + 2 + d], hop((1, -1)[d]))

    spread_unit(hop_a, unit(0, 0), 0)
    spread_unit(hop_b, unit(0, 0), 4)

    t_rows = pl.ds(1 + 4 * c, 4)
    n = 0
    for t, dz in ((0, 0), (1, -1)):
        frames = pl.ds(2 * t, 2)
        for flip in range(2):
            if t == 0 and flip == 0:
                continue
            send(
                target,
                te.at[frames, t_rows],
                t_send.at[n],
                t_recv.at[2 * t + c],
                dev(u, (c + flip) % 2, dz),
            )
            n += 1
        for core in range(2):
            send(
                target.at[:, pl.ds(3 * c, 1)],
                te.at[frames, pl.ds(9 - 9 * c, 1)],
                t_send.at[n],
                t_recv.at[4 + 2 * t + c],
                dev(edge_to, core, dz),
            )
            n += 1

    for d, da in ((0, -1), (1, 1)):
        arrived(weights.at[:, unit(da, 0)], ag_recv.at[d])
        pass_on(hop_a, unit(da, 0), 0, d)
        spread_unit(hop_b, unit(da, 0), 8 + 4 * d)
    for d, db in ((0, -1), (1, 1)):
        arrived(weights.at[:, unit(0, db)], ag_recv.at[4 + d])
        pass_on(hop_b, unit(0, db), 4, d)
    for d in range(2):
        arrived(piece(weights, unit(2, 0), d), ag_recv.at[2 + d])
    spread_unit(hop_b, unit(2, 0), 16)

    xe[2:4, own_rows] = latent[...]
    te[0:2, t_rows] = target[...]
    for t in range(3):
        for core in range(2):
            rows = pl.ds(1 + 2 * core, 2)
            if t == 1:
                rows = pl.ds(1 + 2 * other, 2)
                if core == 1:
                    continue
                arrived(xe.at[pl.ds(2, 2), rows], x_recv.at[2 + other])
            else:
                arrived(xe.at[pl.ds(2 * t, 2), rows], x_recv.at[2 * t + core])
        for core in range(2):
            arrived(xe.at[pl.ds(2 * t, 2), pl.ds(5 - 5 * core, 1)], x_recv.at[6 + 2 * t + core])

    for i, (da, sem) in enumerate(((-1, 8), (1, 12))):
        for d, db in ((0, -1), (1, 1)):
            arrived(weights.at[:, unit(da, db)], ag_recv.at[sem + d])
            pass_on(hop_b, unit(da, db), sem, d)

    @pl.when(u == 0)
    def _():
        xe[:, 0] = jnp.zeros((6, 16, 256), BF16)

    @pl.when(u == 15)
    def _():
        xe[:, 5] = jnp.zeros((6, 16, 256), BF16)

    @pl.when(z == 0)
    def _():
        xe[0:2] = jnp.zeros((2, 6, 16, 256), BF16)

    for a in range(3):
        xc[:, :, :, a * 256 : (a + 1) * 256] = xe[a : a + 4]

    for t in range(2):
        if t == 0:
            arrived(te.at[pl.ds(0, 2), pl.ds(1 + 4 * other, 4)], t_recv.at[other])
        else:
            for core in range(2):
                arrived(te.at[pl.ds(2, 2), pl.ds(1 + 4 * core, 4)], t_recv.at[2 + core])
        for core in range(2):
            arrived(te.at[pl.ds(2 * t, 2), pl.ds(9 - 9 * core, 1)], t_recv.at[4 + 2 * t + core])

    def sort_target(f, carry):
        tf[...] = te[f].astype(F32).reshape(320, 128)
        for i in range(2):
            for j in range(2):
                for r in range(5):
                    row = 2 * r + 1 - i
                    v = tf[pl.ds(row * 32 + j, 16, stride=2), :]
                    tp[f, i, j, r * 16 : (r + 1) * 16, :] = jnp.where(c == 0, v, swap_lanes(v))
        return carry

    lax.fori_loop(0, 4, sort_target, 0)

    for d, db in ((0, -1), (1, 1)):
        arrived(weights.at[:, unit(2, db)], ag_recv.at[16 + d])
        pass_on(hop_b, unit(2, db), 16, d)
    for da, sem in ((0, 4), (-1, 8), (1, 12), (2, 16)):
        for d in range(2):
            arrived(piece(weights, unit(da, 2), d), ag_recv.at[sem + 2 + d])

    zs[...] = jnp.dot(
        xc[...].reshape(384, 768), weights[...].reshape(768, WIDE), preferred_element_type=F32
    ).reshape(4, 96, WIDE)

    def frame(f, loss):
        out = outputs_of([zs[f, :, k * 128 : (k + 1) * 128] for k in range(5)])
        row = lax.broadcasted_iota(jnp.int32, (80, 128), 0)
        keep = jnp.logical_or(f < 2, z < Z - 1)
        keep0 = jnp.logical_and(keep, jnp.logical_or(row < 64, u < 15))
        keep1 = jnp.logical_and(keep, jnp.logical_or(row >= 16, u > 0))
        own = jnp.where(f < 2, 1.0, 0.0)
        g = ([], [])
        for i in range(2):
            for j in range(2):
                misfit = out[i][j] - tp[f, i, j]
                counted = misfit[16 * i : 16 * i + 64]
                loss = loss + own * jnp.sum(counted * counted, axis=0, keepdims=True)
                rounded = misfit.astype(BF16).astype(F32)
                g[i].append(jnp.where((keep0, keep1)[i], rounded, 0.0))
        for k, block in enumerate(folded(g)):
            hs[f, :, k * 128 : (k + 1) * 128] = block.astype(BF16)
        return loss

    loss = lax.fori_loop(0, 4, frame, jnp.zeros((1, 128), F32))
    loss = jnp.where(low_lanes((1, 128)), 0.0, swap_lanes(loss))

    x_t = xe[2:4, 1:5].reshape(128, 256).astype(F32).T.astype(BF16)
    for a in range(3):
        grads = hs[2 - a : 4 - a].reshape(128, WIDE)
        part = jnp.dot(x_t, grads, preferred_element_type=F32)
        if a == 0:
            dw[0, :, :, 0:512] = part[:, 0:512].astype(BF16).reshape(16, 16, 512)
            dw[0, :, :, 512:WIDE] = (part[:, 512:WIDE] + loss).astype(BF16).reshape(16, 16, 128)
        else:
            dw[a] = part.astype(BF16).reshape(16, 16, WIDE)

    def open_ring(hop, units, far, near, slot, sem):
        far_unit, plus, minus = units
        for d, step in enumerate((1, -1)):
            first_col, width = PARTS[d]
            send(
                piece(dw, far_unit, d),
                far.at[slot, :, :, pl.ds(first_col, width)],
                rs_send.at[sem + d],
                rs_recv.at[sem + d],
                hop(step),
            )
        for d, (step, index) in enumerate(((1, plus), (-1, minus))):
            first_col, width = PARTS[1 - d]
            send(
                piece(dw, index, 1 - d),
                near.at[slot, d, :, :, pl.ds(first_col, width)],
                rs_send.at[sem + 2 + d],
                rs_recv.at[sem + 2 + d],
                hop(step),
            )

    def add_far(hop, units, far, near, slot, sem):
        _, plus, minus = units
        for d, (step, index) in enumerate(((1, plus), (-1, minus))):
            first_col, width = PARTS[d]
            cols = pl.ds(first_col, width)
            arrived(far.at[slot, :, :, cols], rs_recv.at[sem + d])
            dw[:, index, :, cols] = (
                dw[:, index, :, cols].astype(F32) + far[slot, :, :, cols].astype(F32)
            ).astype(BF16)
            send(
                piece(dw, index, d),
                near.at[slot, d, :, :, cols],
                rs_send.at[sem + 4 + d],
                rs_recv.at[sem + 4 + d],
                hop(step),
            )

    def close_ring(index, near, slot, sem):
        for d in range(2):
            for early in range(2):
                first_col, width = PARTS[1 - d if early else d]
                arrived(
                    near.at[slot, d, :, :, pl.ds(first_col, width)],
                    rs_recv.at[sem + (2 if early else 4) + d],
                )
        return (
            dw[:, index].astype(F32) + near[slot, 0].astype(F32) + near[slot, 1].astype(F32)
        )

    order = (2, 1, -1, 0)
    rings = [(unit(k, 2), unit(k, 1), unit(k, -1)) for k in order]
    for i in range(4):
        open_ring(hop_b, rings[i], far_b, near_b, i, 6 * i)

    lat = jnp.zeros((128, 256), F32)
    for a in range(3):
        lat = lat + lax.dot_general(
            hs[2 - a : 4 - a].reshape(128, WIDE),
            weights[a].reshape(256, WIDE),
            (((1,), (1,)), ((), ())),
            preferred_element_type=F32,
        )
    lat = lat.reshape(2, 4, 16, 256)
    lat_out[...] = jnp.where(c == 0, lat[:, 2:4], lat[:, 0:2])
    lat_own[...] = jnp.where(c == 0, lat[:, 0:2], lat[:, 2:4])
    send(lat_out, lat_in, lat_sem.at[0], lat_sem.at[1], sibling)

    for i in range(4):
        add_far(hop_b, rings[i], far_b, near_b, i, 6 * i)
    for i in range(3):
        dw[:, unit(order[i], 0)] = close_ring(unit(order[i], 0), near_b, i, 6 * i).astype(BF16)
    ring_a = (unit(2, 0), unit(1, 0), unit(-1, 0))
    open_ring(hop_a, ring_a, far_a, near_a, 0, 24)
    dw[:, unit(0, 0)] = close_ring(unit(0, 0), near_b, 3, 18).astype(BF16)
    add_far(hop_a, ring_a, far_a, near_a, 0, 24)
    total[...] = close_ring(unit(0, 0), near_a, 0, 24)

    for p in range(15):
        a, k = p // 5, p % 5
        zsend_buf[p] = total[a, :, k * 128 : (k + 1) * 128].astype(BF16)
    zsend_buf[15] = jnp.zeros((16, 128), BF16)

    def z_copy(i):
        to = (z + i) % Z
        return remote(zsend_buf.at[to], zrecv_buf.at[z], z_send.at[i], z_recv.at[z], (to, h))

    def z_start(i, carry):
        z_copy(i).start()
        return carry

    lax.fori_loop(1, Z, z_start, 0)

    def z_add(i, acc):
        source = (z + i) % Z
        arrived(zrecv_buf.at[source], z_recv.at[source])
        return acc + zrecv_buf[source].astype(F32)

    acc = lax.fori_loop(1, Z, z_add, zsend_buf[z].astype(F32))
    for core in range(2):
        gsend_buf[core] = acc[8 * core : 8 * core + 8]
    grecv_buf[c, z] = gsend_buf[c]

    def g_copy(i):
        core = (c + i % 2) % 2
        return remote(
            gsend_buf.at[core],
            grecv_buf.at[c, z],
            g_send.at[i],
            g_recv.at[c * Z + z],
            dev(u, core, i // 2),
        )

    def g_start(i, carry):
        g_copy(i).start()
        return carry

    lax.fori_loop(1, 2 * Z, g_start, 0)

    arrived(lat_in, lat_sem.at[1])
    out_latent[...] = (lat_own[...] + lat_in[...]).astype(BF16)
    for load in loads:
        load.wait()

    def g_wait(i, carry):
        core = (c + i % 2) % 2
        source = (z + i // 2) % Z
        arrived(grecv_buf.at[core, source], g_recv.at[core * Z + source])
        return carry

    lax.fori_loop(1, 2 * Z, g_wait, 0)

    low = low_lanes((8, 128))
    for a in range(3):
        for k in range(5):
            b0, b1 = grecv_buf[0, 5 * a + k], grecv_buf[1, 5 * a + k]
            pair = (jnp.where(low, b0, swap_lanes(b1)), jnp.where(low, swap_lanes(b0), b1))
            for s in range(2):
                if 2 * k + s == 9:
                    if a == 0:
                        whole = jnp.where(low, 0.0, b0 + b1)[0:1]
                        out_loss[0, 0] = jnp.sum(whole) * (1.0 / 16777216)
                    continue
                cols = pl.ds((9 * a + 2 * k + s) * 128, 128)
                values = adam(
                    SCALE * pair[s], master[:, cols], first[:, cols], second[:, cols], ema[:, cols]
                )
                for ref, value in zip((out_master, out_first, out_second, out_ema), values):
                    ref[:, cols] = value

    for copy in sent:
        copy.wait_send()

    def z_done(i, carry):
        z_copy(i).wait_send()
        return carry

    def g_done(i, carry):
        g_copy(i).wait_send()
        return carry

    lax.fori_loop(1, Z, z_done, 0)
    lax.fori_loop(1, 2 * Z, g_done, 0)


def per_device(latent, target_frames, master, first_moment, second_moment, ema_weights):
    vmem = pl.BlockSpec(memory_space=pltpu.VMEM)
    hbm = pl.BlockSpec(memory_space=pl.ANY)
    state = jax.ShapeDtypeStruct(master.shape, F32)
    dma = pltpu.SemaphoreType.DMA
    outs = pl.pallas_call(
        kernel,
        out_shape=(
            state,
            state,
            state,
            state,
            jax.ShapeDtypeStruct(latent.shape, BF16),
            jax.ShapeDtypeStruct((1, 1), F32),
        ),
        in_specs=[vmem, vmem, vmem, hbm, hbm, hbm],
        out_specs=(vmem, vmem, vmem, vmem, vmem, pl.BlockSpec(memory_space=pltpu.SMEM)),
        scratch_shapes=[
            pltpu.VMEM((3, 8, WIDE), F32),
            pltpu.VMEM((3, 8, WIDE), F32),
            pltpu.VMEM((3, 16, 16, WIDE), BF16),
            pltpu.VMEM((6, 6, 16, 256), BF16),
            pltpu.VMEM((4, 6, 16, 768), BF16),
            pltpu.VMEM((4, 10, 32, 128), BF16),
            pltpu.VMEM((320, 128), F32),
            pltpu.VMEM((4, 2, 2, 80, 128), F32),
            pltpu.VMEM((4, 96, WIDE), F32),
            pltpu.VMEM((4, 64, WIDE), BF16),
            pltpu.VMEM((3, 16, 16, WIDE), BF16),
            pltpu.VMEM((4, 3, 16, WIDE), BF16),
            pltpu.VMEM((4, 2, 3, 16, WIDE), BF16),
            pltpu.VMEM((1, 3, 16, WIDE), BF16),
            pltpu.VMEM((1, 2, 3, 16, WIDE), BF16),
            pltpu.VMEM((3, 16, WIDE), F32),
            pltpu.VMEM((16, 16, 128), BF16),
            pltpu.VMEM((16, 16, 128), BF16),
            pltpu.VMEM((2, 8, 128), F32),
            pltpu.VMEM((2, 16, 8, 128), F32),
            pltpu.VMEM((2, 2, 16, 256), F32),
            pltpu.VMEM((2, 2, 16, 256), F32),
            pltpu.VMEM((2, 2, 16, 256), F32),
            pltpu.VMEM((8, 3456), F32),
            pltpu.VMEM((8, 3456), F32),
            pltpu.VMEM((8, 3456), F32),
            dma((2,)),
            dma((20,)),
            dma((20,)),
            dma((11,)),
            dma((12,)),
            dma((7,)),
            dma((8,)),
            dma((30,)),
            dma((30,)),
            dma((16,)),
            dma((16,)),
            dma((32,)),
            dma((32,)),
            dma((2,)),
            dma((3,)),
        ],
        compiler_params=pltpu.CompilerParams(
            collective_id=0, has_side_effects=True, vmem_limit_bytes=40 * 1024 * 1024
        ),
    )(latent, target_frames, master, first_moment, second_moment, ema_weights)
    return (*outs[:5], outs[5].reshape(()))


def solution(mesh):
    placed = (
        P("tm", "height", None, None),
        P("tm", "height", None, None),
        P("height", None),
        P("height", None),
        P("height", None),
        P("height", None),
    )
    return jax.shard_map(
        per_device,
        mesh=mesh,
        in_specs=placed,
        out_specs=(
            P("height", None),
            P("height", None),
            P("height", None),
            P("height", None),
            P("tm", "height", None, None),
            P(),
        ),
        check_vma=False,
    )
```

time: 399 us -> 83.1 us (0.21)
  the two profiles are of different devices: /device:TPU:2 before, /device:TPU:1 now
where the time goes in v1:
time: 83.1 us; the launch traced here: 82.8 us
  Pallas kernels  71.9 us (87%)
  local copies, waits for them, and re-layouts  8.37 us (10%)
  between operations  2.48 us (3%)
    pallas_call x1, Pallas kernels, per_device(): pl.pallas_call(kernel, out_shape=(state, state, state, state, jax.ShapeDt...  71.9 us
    unnamed x17, local copies, waits for them, and re-layouts  8.37 us

profile of v1, /device:TPU:1, one launch (start us, length us, event | category | flops | bytes accessed | tf_op | source)
XLA Modules:
  0.0 82.8 jit_solution(7070614623624273808)
XLA Ops:
  0.6 0.0 copy-start
  0.6 0.9 %copy-done = f32[8,3456]{1,0:T(8,128)S(1)} copy-done((f32[8,3456]{1,0:T(8,128)S(1)}, f32[8,3456]{1,0:T(8,128)}, u32[]{:S(2)}) %copy-start) | copy-done | bytes 110616
  1.5 0.0 copy-start.1
  1.5 0.9 %copy-done.1 = f32[8,3456]{1,0:T(8,128)S(1)} copy-done((f32[8,3456]{1,0:T(8,128)S(1)}, f32[8,3456]{1,0:T(8,128)}, u32[]{:S(2)}) %copy-start.1) | copy-done | bytes 110616
  2.4 0.0 copy-start.2
  2.4 0.9 %copy-done.2 = f32[8,3456]{1,0:T(8,128)S(1)} copy-done((f32[8,3456]{1,0:T(8,128)S(1)}, f32[8,3456]{1,0:T(8,128)}, u32[]{:S(2)}) %copy-start.2) | copy-done | bytes 110616
  3.3 0.0 copy-start.3
  3.3 0.9 %copy-done.3 = f32[8,3456]{1,0:T(8,128)S(1)} copy-done((f32[8,3456]{1,0:T(8,128)S(1)}, f32[8,3456]{1,0:T(8,128)}, u32[]{:S(2)}) %copy-start.3) | copy-done | bytes 110616
  4.2 0.0 copy-start.4
  4.2 0.8 %copy-done.4 = bf16[2,4,32,128]{3,2,1,0:T(8,128)(2,1)S(1)} copy-done((bf16[2,4,32,128]{3,2,1,0:T(8,128)(2,1)S(1)}, bf16[2,4,32,128]{3,2,1,0:T(8,128)(2,1)}, u32[]{:S(2)}) %copy-start.4) | copy-done | bytes 65560
  5.1 0.0 copy-start.5
  5.1 0.8 copy-done.5
  5.8 71.9 %shard_map.109 = (f32[8,3456]{1,0:T(8,128)S(1)}, f32[8,3456]{1,0:T(8,128)S(1)}, f32[8,3456]{1,0:T(8,128)S(1)}, f32[8,3456]{1,0:T(8,128)S(1)}, bf16[2,2,16,256]{3,2,1,0:T(8,128)(2,1)S(1)}, /*index=5*/f32[1,1]{1,0:T(1,128)}) custom-call(bf16[2,2,16,256]{3,2,1,0:T(8,128)(2,1)S(1)} %copy-done.5, bf16[2,4,32,128]{3,2,1,0:T(8,128)(2,1)S(1)} %copy-done.4, ...), custom_call_target="tpu_custom_call" | custom-call | tf_op jit(solution)/shard_map/pallas_call | solution.py:596
  77.8 0.6 copy.18
  78.4 0.6 copy.19
  79.1 0.6 copy.20
  79.7 0.6 copy.21
  80.4 0.6 copy.22
Async XLA Ops:
  0.6 0.9 %copy-start = (f32[8,3456]{1,0:T(8,128)S(1)}, f32[8,3456]{1,0:T(8,128)}, u32[]{:S(2)}) copy-start(f32[8,3456]{1,0:T(8,128)} %master.1) | copy-start | bytes 331780
  1.5 0.9 %copy-start.1 = (f32[8,3456]{1,0:T(8,128)S(1)}, f32[8,3456]{1,0:T(8,128)}, u32[]{:S(2)}) copy-start(f32[8,3456]{1,0:T(8,128)} %first_hbm.1) | copy-start | bytes 331780
  2.4 0.9 %copy-start.2 = (f32[8,3456]{1,0:T(8,128)S(1)}, f32[8,3456]{1,0:T(8,128)}, u32[]{:S(2)}) copy-start(f32[8,3456]{1,0:T(8,128)} %second_hbm.1) | copy-start | bytes 331780
  3.3 0.9 %copy-start.3 = (f32[8,3456]{1,0:T(8,128)S(1)}, f32[8,3456]{1,0:T(8,128)}, u32[]{:S(2)}) copy-start(f32[8,3456]{1,0:T(8,128)} %ema_hbm.1) | copy-start | bytes 331780
  4.2 0.8 %copy-start.4 = (bf16[2,4,32,128]{3,2,1,0:T(8,128)(2,1)S(1)}, bf16[2,4,32,128]{3,2,1,0:T(8,128)(2,1)}, u32[]{:S(2)}) copy-start(bf16[2,4,32,128]{3,2,1,0:T(8,128)(2,1)} %target.1) | copy-start | bytes 196612
  5.1 0.8 copy-start.5

commit v2 on v1

v2 whole, which is shorter than its diff:
```python
import math

import jax
import jax.numpy as jnp
from jax import lax
from jax.experimental import pallas as pl
from jax.experimental.pallas import tpu as pltpu
from jax.sharding import PartitionSpec as P

learn_rate = 0.3
beta_first = 0.9
beta_second = 0.99
ema_decay = 0.9
adam_eps = 1e-08

MESH = pl.DeviceIdType.MESH
F32 = jnp.float32
BF16 = jnp.bfloat16
SCALE = 1.0 / math.sqrt(27 * 256)
WIDE = 640
Z = 16


def low_lanes(shape):
    return lax.broadcasted_iota(jnp.int32, shape, len(shape) - 1) < 64


def swap_lanes(v):
    return pltpu.roll(v, 64, axis=v.ndim - 1)


def col_of(shape):
    return lax.broadcasted_iota(jnp.int32, shape, 0) % 16


def from_left(v):
    return jnp.where(col_of(v.shape) == 0, 0.0, pltpu.roll(v, 1, axis=0))


def from_right(v):
    return jnp.where(col_of(v.shape) == 15, 0.0, pltpu.roll(v, v.shape[0] - 1, axis=0))


def split_halves(m):
    low = low_lanes((8, 128))
    zero = jnp.zeros((8, 128), F32)
    halves = ([], [])
    for a in range(3):
        blocks = ([], [])
        for k in range(5):
            t = 9 * a + 2 * k
            even = m[:, t * 128 : (t + 1) * 128]
            odd = m[:, (t + 1) * 128 : (t + 2) * 128] if k < 4 else zero
            blocks[0].append(jnp.where(low, even, swap_lanes(odd)))
            blocks[1].append(jnp.where(low, swap_lanes(even), odd))
        for c in range(2):
            halves[c].append(jnp.concatenate(blocks[c], axis=1))
    return halves


def slot_of(blocks, s):
    return swap_lanes(blocks[s // 2]) if s % 2 else blocks[s // 2]


def outputs_of(z):
    u = []
    for b in range(3):
        z0, z1, z2 = (slot_of(z, 3 * b + e) for e in range(3))
        u.append((from_left(z0) + z1 + z2, z0 + z1 + from_right(z2)))
    out = ([], [])
    for j in range(2):
        common = u[0][j][0:80] + u[2][j][16:96]
        out[0].append(common + u[1][j][16:96])
        out[1].append(common + u[1][j][0:80])
    return out


def folded(g):
    slots = []
    for b in range(3):
        v = []
        for j in range(2):
            g0, g1 = g[0][j], g[1][j]
            v.append((g1[16:80] + g0[16:80], g0[0:64] + g1[16:80], g1[0:64] + g0[0:64])[b])
        slots += [v[1] + from_right(v[0]), v[0] + v[1], from_left(v[1]) + v[0]]
    low = low_lanes((64, 128))
    blocks = []
    for k in range(5):
        odd = swap_lanes(slots[2 * k + 1]) if k < 4 else jnp.zeros((64, 128), F32)
        blocks.append(jnp.where(low, slots[2 * k], odd))
    return blocks


def remote(src, dst, send_sem, recv_sem, device):
    return pltpu.make_async_remote_copy(
        src_ref=src,
        dst_ref=dst,
        send_sem=send_sem,
        recv_sem=recv_sem,
        device_id=device,
        device_id_type=MESH,
    )


def kernel(
    latent,
    target,
    master,
    out_grad,
    out_own,
    out_other,
    out_loss,
    own_kernel,
    pair_out,
    pair_in,
    weights,
    xe,
    xc,
    te,
    tf,
    tp,
    zs,
    hs,
    dw,
    got_b,
    part_b,
    got_a,
    swap_out,
    swap_in,
    zsend_buf,
    zrecv_buf,
    gsend_buf,
    grecv_buf,
    lat_out,
    pair_sem,
    ag_send,
    ag_recv,
    x_send,
    x_recv,
    t_send,
    t_recv,
    rb_send,
    rb_recv,
    ra_send,
    ra_recv,
    swap_sem,
    z_send,
    z_recv,
    g_send,
    g_recv,
    lat_sem,
    load_sem,
):
    z = lax.axis_index("tm")
    h = lax.axis_index("height")
    c = h % 2
    u = h // 2
    other = 1 - c
    sa, sb = 4 - 3 * c, 1 + 3 * c
    pa = jnp.where(c == 0, u // 4, u % 4)
    pb = jnp.where(c == 0, u % 4, u // 4)

    def unit(da, db):
        return ((pa + da) % 4) * sa + ((pb + db) % 4) * sb

    def dev(chip, core, dz=0):
        return ((z + dz + Z) % Z, chip * 2 + core)

    sibling = dev(u, other)
    above, below = (u + 15) % 16, (u + 1) % 16
    own_rows = pl.ds(1 + 2 * c, 2)
    t_rows = pl.ds(1 + 4 * c, 4)

    loads = [
        pltpu.make_async_copy(src, dst, load_sem.at[i])
        for i, (src, dst) in enumerate(
            ((master, own_kernel), (latent, xe.at[2:4, own_rows]), (target, te.at[0:2, t_rows]))
        )
    ]
    for load in loads:
        load.start()

    barrier = pltpu.get_barrier_semaphore()
    peers = [sibling]
    for j in range(1, 4):
        peers += [dev(unit(j, 0), c), dev(unit(0, j), c)]
    for dz in (-1, 0, 1):
        for chip in (above, below):
            for core in range(2):
                peers.append(dev(chip, core, dz))
        if dz:
            peers.append(dev(u, other, dz))
    for peer in peers:
        pl.semaphore_signal(barrier, inc=1, device_id=peer, device_id_type=MESH)

    def greet(i, carry):
        pl.semaphore_signal(barrier, inc=1, device_id=((z + i) % Z, h), device_id_type=MESH)
        return carry

    lax.fori_loop(1, Z, greet, 0)

    loads[0].wait()
    halves = split_halves(own_kernel[...] * SCALE)
    for a in range(3):
        pair_out[a] = jnp.where(c == 0, halves[1][a], halves[0][a])

    pl.semaphore_wait(barrier, len(peers) + Z - 1)

    sent = []

    def send(*args):
        copy = remote(*args)
        copy.start()
        sent.append(copy)

    def arrived(dst, sem):
        remote(dst, dst, ag_send.at[0], sem, sibling).wait_recv()

    send(pair_out, pair_in, pair_sem.at[0], pair_sem.at[1], sibling)

    edge = pl.ds(c, 1)
    edge_to = jnp.where(c == 0, above, below)
    edge_row = pl.ds(5 - 5 * c, 1)

    def send_latent():
        n = 0
        for t, dz in ((0, 1), (1, 0), (2, -1)):
            frames = pl.ds(2 * t, 2)
            for flip in range(2):
                if t == 1 and flip == 0:
                    continue
                send(
                    latent,
                    xe.at[frames, own_rows],
                    x_send.at[n],
                    x_recv.at[2 * t + c],
                    dev(u, (c + flip) % 2, dz),
                )
                n += 1
        for t, dz in ((0, 1), (1, 0), (2, -1)):
            frames = pl.ds(2 * t, 2)
            for core in range(2):
                send(
                    latent.at[:, edge],
                    xe.at[frames, edge_row],
                    x_send.at[n],
                    x_recv.at[6 + 2 * t + c],
                    dev(edge_to, core, dz),
                )
                n += 1

    def send_target():
        n = 0
        for t, dz in ((0, 0), (1, -1)):
            frames = pl.ds(2 * t, 2)
            for flip in range(2):
                if t == 0 and flip == 0:
                    continue
                send(
                    target,
                    te.at[frames, t_rows],
                    t_send.at[n],
                    t_recv.at[2 * t + c],
                    dev(u, (c + flip) % 2, dz),
                )
                n += 1
            for core in range(2):
                send(
                    target.at[:, pl.ds(3 * c, 1)],
                    te.at[frames, pl.ds(9 - 9 * c, 1)],
                    t_send.at[n],
                    t_recv.at[4 + 2 * t + c],
                    dev(edge_to, core, dz),
                )
                n += 1

    arrived(pair_in, pair_sem.at[1])
    for a in range(3):
        mine = jnp.where(c == 0, halves[0][a], halves[1][a])
        theirs = pair_in[a]
        rows = jnp.concatenate(
            [jnp.where(c == 0, mine, theirs), jnp.where(c == 0, theirs, mine)], axis=0
        )
        weights[a, u] = rows.astype(BF16)

    def send_unit(index, sem, to):
        place = weights.at[:, index]
        send(place, place, ag_send.at[sem], ag_recv.at[sem], dev(to, c))

    far_first = (2, 1, 3)
    for j in far_first:
        send_unit(u, j - 1, unit(j, 0))
    for j in far_first:
        send_unit(u, 2 + j, unit(0, j))
    send_latent()
    for k in (1, 3, 2):
        index = unit(4 - k, 0)
        arrived(weights.at[:, index], ag_recv.at[k - 1])
        for j in far_first:
            send_unit(index, 2 + 3 * k + j, unit(0, j))
    send_target()

    for load in loads[1:]:
        load.wait()
    for t in range(3):
        for core in range(2):
            rows = pl.ds(1 + 2 * core, 2)
            if t == 1:
                rows = pl.ds(1 + 2 * other, 2)
                if core == 1:
                    continue
                arrived(xe.at[pl.ds(2, 2), rows], x_recv.at[2 + other])
            else:
                arrived(xe.at[pl.ds(2 * t, 2), rows], x_recv.at[2 * t + core])
        for core in range(2):
            arrived(xe.at[pl.ds(2 * t, 2), pl.ds(5 - 5 * core, 1)], x_recv.at[6 + 2 * t + core])

    @pl.when(u == 0)
    def _():
        xe[:, 0] = jnp.zeros((6, 16, 256), BF16)

    @pl.when(u == 15)
    def _():
        xe[:, 5] = jnp.zeros((6, 16, 256), BF16)

    @pl.when(z == 0)
    def _():
        xe[0:2] = jnp.zeros((2, 6, 16, 256), BF16)

    for a in range(3):
        xc[:, :, :, a * 256 : (a + 1) * 256] = xe[a : a + 4]
    x_t = xe[2:4, 1:5].reshape(128, 256).astype(F32).T.astype(BF16)

    for t in range(2):
        if t == 0:
            arrived(te.at[pl.ds(0, 2), pl.ds(1 + 4 * other, 4)], t_recv.at[other])
        else:
            for core in range(2):
                arrived(te.at[pl.ds(2, 2), pl.ds(1 + 4 * core, 4)], t_recv.at[2 + core])
        for core in range(2):
            arrived(te.at[pl.ds(2 * t, 2), pl.ds(9 - 9 * core, 1)], t_recv.at[4 + 2 * t + core])

    def sort_target(f, carry):
        tf[...] = te[f].astype(F32).reshape(320, 128)
        for i in range(2):
            for j in range(2):
                for r in range(5):
                    row = 2 * r + 1 - i
                    v = tf[pl.ds(row * 32 + j, 16, stride=2), :]
                    tp[f, i, j, r * 16 : (r + 1) * 16, :] = jnp.where(c == 0, v, swap_lanes(v))
        return carry

    lax.fori_loop(0, 4, sort_target, 0)

    for k in (0, 3, 1, 2):
        for j in far_first:
            arrived(weights.at[:, unit(4 - k, 4 - j)], ag_recv.at[2 + 3 * k + j])

    zs[...] = jnp.dot(
        xc[...].reshape(384, 768), weights[...].reshape(768, WIDE), preferred_element_type=F32
    ).reshape(4, 96, WIDE)

    def frame(f, loss):
        out = outputs_of([zs[f, :, k * 128 : (k + 1) * 128] for k in range(5)])
        row = lax.broadcasted_iota(jnp.int32, (80, 128), 0)
        keep = jnp.logical_or(f < 2, z < Z - 1)
        keep0 = jnp.logical_and(keep, jnp.logical_or(row < 64, u < 15))
        keep1 = jnp.logical_and(keep, jnp.logical_or(row >= 16, u > 0))
        own = jnp.where(f < 2, 1.0, 0.0)
        g = ([], [])
        for i in range(2):
            for j in range(2):
                misfit = out[i][j] - tp[f, i, j]
                counted = misfit[16 * i : 16 * i + 64]
                loss = loss + own * jnp.sum(counted * counted, axis=0, keepdims=True)
                rounded = misfit.astype(BF16).astype(F32)
                g[i].append(jnp.where((keep0, keep1)[i], rounded, 0.0))
        for k, block in enumerate(folded(g)):
            hs[f, :, k * 128 : (k + 1) * 128] = block.astype(BF16)
        return loss

    loss = lax.fori_loop(0, 4, frame, jnp.zeros((1, 128), F32))
    loss = jnp.where(low_lanes((1, 128)), 0.0, swap_lanes(loss))

    for a in range(3):
        grads = hs[2 - a : 4 - a].reshape(128, WIDE)
        part = jnp.dot(x_t, grads, preferred_element_type=F32)
        for v in range(16):
            rows = part[16 * v : 16 * v + 16]
            in_b = jnp.where(c == 0, v % 4, v // 4)
            in_a = jnp.where(c == 0, v // 4, v % 4)
            if a == 0:
                dw[a, in_b, in_a, :, 0:512] = rows[:, 0:512].astype(BF16)
                dw[a, in_b, in_a, :, 512:WIDE] = (rows[:, 512:WIDE] + loss).astype(BF16)
            else:
                dw[a, in_b, in_a] = rows.astype(BF16)
        for j in far_first:
            sem = 3 * a + j - 1
            send(
                dw.at[a, (pb + j) % 4],
                got_b.at[a, j - 1],
                rb_send.at[sem],
                rb_recv.at[sem],
                dev(unit(0, j), c),
            )

    lat = jnp.zeros((128, 256), F32)
    for a in range(3):
        lat = lat + lax.dot_general(
            hs[2 - a : 4 - a].reshape(128, WIDE),
            weights[a].reshape(256, WIDE),
            (((1,), (1,)), ((), ())),
            preferred_element_type=F32,
        )
    lat = lat.reshape(2, 4, 16, 256)
    lat_out[...] = jnp.where(c == 0, lat[:, 2:4], lat[:, 0:2])
    out_own[...] = jnp.where(c == 0, lat[:, 0:2], lat[:, 2:4])
    send(lat_out, out_other, lat_sem.at[0], lat_sem.at[1], sibling)

    for a in range(3):
        for j in range(1, 4):
            arrived(got_b.at[a, j - 1], rb_recv.at[3 * a + j - 1])
        for k in far_first + (0,):
            at = (pa + k) % 4
            rows = dw[a, pb, at].astype(F32)
            for j in range(3):
                rows = rows + got_b[a, j, at].astype(F32)
            part_b[a, k] = rows.astype(BF16)
            if k:
                sem = 3 * a + k - 1
                send(
                    part_b.at[a, k],
                    got_a.at[a, k - 1],
                    ra_send.at[sem],
                    ra_recv.at[sem],
                    dev(unit(k, 0), c),
                )

    totals = []
    for a in range(3):
        rows = part_b[a, 0].astype(F32)
        for j in range(1, 4):
            arrived(got_a.at[a, j - 1], ra_recv.at[3 * a + j - 1])
            rows = rows + got_a[a, j - 1].astype(F32)
        swap_out[a] = jnp.where(c == 0, rows[8:16], rows[0:8])
        totals.append(jnp.where(c == 0, rows[0:8], rows[8:16]))
    send(swap_out, swap_in, swap_sem.at[0], swap_sem.at[1], sibling)
    arrived(swap_in, swap_sem.at[1])

    for a in range(3):
        theirs = swap_in[a]
        rows = jnp.concatenate(
            [jnp.where(c == 0, totals[a], theirs), jnp.where(c == 0, theirs, totals[a])], axis=0
        ).astype(BF16)
        for k in range(5):
            zsend_buf[5 * a + k] = rows[:, k * 128 : (k + 1) * 128]
    zsend_buf[15] = jnp.zeros((16, 128), BF16)

    def z_copy(i):
        to = (z + i) % Z
        return remote(zsend_buf.at[to], zrecv_buf.at[z], z_send.at[i], z_recv.at[z], (to, h))

    def g_copy(i):
        to = (z + i) % Z
        return remote(gsend_buf, grecv_buf.at[z], g_send.at[i], g_recv.at[z], (to, h))

    order = [8] + [v for d in range(7, 0, -1) for v in (d, 16 - d)]
    for i in order:
        z_copy(i).start()

    acc = zsend_buf[z].astype(F32)
    for i in reversed(order):
        source = (z + i) % Z
        arrived(zrecv_buf.at[source], z_recv.at[source])
        acc = acc + zrecv_buf[source].astype(F32)
    gsend_buf[...] = acc.astype(BF16)
    for i in order:
        g_copy(i).start()
    grecv_buf[z] = gsend_buf[...]
    arrived(out_other, lat_sem.at[1])
    for copy in sent:
        copy.wait_send()
    for i in order:
        z_copy(i).wait_send()
    for i in reversed(order):
        source = (z + i) % Z
        arrived(grecv_buf.at[source], g_recv.at[source])

    low = low_lanes((8, 128))
    for a in range(3):
        for k in range(5):
            both = grecv_buf[5 * a + k].astype(F32)
            b0, b1 = both[0:8], both[8:16]
            pair = (jnp.where(low, b0, swap_lanes(b1)), jnp.where(low, swap_lanes(b0), b1))
            for s in range(2):
                if 2 * k + s < 9:
                    t = 9 * a + 2 * k + s
                    out_grad[:, t * 128 : (t + 1) * 128] = SCALE * pair[s]
                elif a == 0:
                    whole = jnp.where(low, 0.0, b0 + b1)[0:1]
                    out_loss[0, 0] = jnp.sum(whole) * (1.0 / 16777216)

    for i in order:
        g_copy(i).wait_send()


def per_device(latent, target_frames, master, first_moment, second_moment, ema_weights):
    vmem = pl.BlockSpec(memory_space=pltpu.VMEM)
    hbm = pl.BlockSpec(memory_space=pltpu.HBM)
    dma = pltpu.SemaphoreType.DMA
    half_grad = jax.ShapeDtypeStruct(latent.shape, F32)
    grad, own, other, loss = pl.pallas_call(
        kernel,
        out_shape=(
            jax.ShapeDtypeStruct(master.shape, F32),
            half_grad,
            half_grad,
            jax.ShapeDtypeStruct((1, 1), F32),
        ),
        in_specs=[hbm, hbm, hbm],
        out_specs=(vmem, vmem, vmem, pl.BlockSpec(memory_space=pltpu.SMEM)),
        scratch_shapes=[
            pltpu.VMEM((8, 3456), F32),
            pltpu.VMEM((3, 8, WIDE), F32),
            pltpu.VMEM((3, 8, WIDE), F32),
            pltpu.VMEM((3, 16, 16, WIDE), BF16),
            pltpu.VMEM((6, 6, 16, 256), BF16),
            pltpu.VMEM((4, 6, 16, 768), BF16),
            pltpu.VMEM((4, 10, 32, 128), BF16),
            pltpu.VMEM((320, 128), F32),
            pltpu.VMEM((4, 2, 2, 80, 128), F32),
            pltpu.VMEM((4, 96, WIDE), F32),
            pltpu.VMEM((4, 64, WIDE), BF16),
            pltpu.VMEM((3, 4, 4, 16, WIDE), BF16),
            pltpu.VMEM((3, 3, 4, 16, WIDE), BF16),
            pltpu.VMEM((3, 4, 16, WIDE), BF16),
            pltpu.VMEM((3, 3, 16, WIDE), BF16),
            pltpu.VMEM((3, 8, WIDE), F32),
            pltpu.VMEM((3, 8, WIDE), F32),
            pltpu.VMEM((16, 16, 128), BF16),
            pltpu.VMEM((16, 16, 128), BF16),
            pltpu.VMEM((16, 128), BF16),
            pltpu.VMEM((16, 16, 128), BF16),
            pltpu.VMEM((2, 2, 16, 256), F32),
            dma((2,)),
            dma((15,)),
            dma((15,)),
            dma((11,)),
            dma((12,)),
            dma((7,)),
            dma((8,)),
            dma((9,)),
            dma((9,)),
            dma((9,)),
            dma((9,)),
            dma((2,)),
            dma((16,)),
            dma((16,)),
            dma((16,)),
            dma((16,)),
            dma((2,)),
            dma((3,)),
        ],
        compiler_params=pltpu.CompilerParams(
            collective_id=0, has_side_effects=True, vmem_limit_bytes=40 * 1024 * 1024
        ),
    )(latent, target_frames, master)
    new_first = beta_first * first_moment + (1.0 - beta_first) * grad
    new_second = beta_second * second_moment + (1.0 - beta_second) * grad * grad
    new_master = master - learn_rate * new_first / (jnp.sqrt(new_second) + adam_eps)
    new_ema = ema_decay * ema_weights + (1.0 - ema_decay) * new_master
    latent_grad = (own + other).astype(BF16)
    return (new_master, new_first, new_second, new_ema, latent_grad, loss.reshape(()))


def solution(mesh):
    placed = (
        P("tm", "height", None, None),
        P("tm", "height", None, None),
        P("height", None),
        P("height", None),
        P("height", None),
        P("height", None),
    )
    return jax.shard_map(
        per_device,
        mesh=mesh,
        in_specs=placed,
        out_specs=(
            P("height", None),
            P("height", None),
            P("height", None),
            P("height", None),
            P("tm", "height", None, None),
            P(),
        ),
        check_vma=False,
    )
```

time: 83.1 us -> 69.3 us (0.83)
  Pallas kernels: 71.9 us -> 62.5 us
  local copies, waits for them, and re-layouts: 8.37 us -> 2.77 us
  other arithmetic: 0 us -> 1.42 us
    pallas_call x1, Pallas kernels: 71.9 us -> 62.5 us  [per_device(): pl.pallas_call(kernel, out_shape=(jax.ShapeDtypeStruct(master.shape, F32)...]
    unnamed x17 -> x12, local copies, waits for them, and re-layouts: 8.37 us -> 2.77 us
where the time goes in v2:
time: 69.3 us; the launch traced here: 69 us
  Pallas kernels  62.5 us (90%)
  local copies, waits for them, and re-layouts  2.77 us (4%)
  between operations  2.35 us (3%)
  other arithmetic  1.42 us (2%)
    pallas_call x1, Pallas kernels, per_device(): pl.pallas_call(kernel, out_shape=(jax.ShapeDtypeStruct(master.shape, F32)...  62.5 us
    unnamed x12, local copies, waits for them, and re-layouts  2.77 us

profile of v2, /device:TPU:1, one launch (start us, length us, event | category | flops | bytes accessed | tf_op | source)
XLA Modules:
  0.0 69.0 jit_solution(7421190149000458558)
XLA Ops:
  0.6 0.0 copy-start
  0.6 0.9 %copy-done = f32[8,3456]{1,0:T(8,128)S(1)} copy-done((f32[8,3456]{1,0:T(8,128)S(1)}, f32[8,3456]{1,0:T(8,128)}, u32[]{:S(2)}) %copy-start) | copy-done | bytes 110616
  1.5 0.0 copy-start.1
  1.5 0.8 %copy-done.1 = bf16[2,4,32,128]{3,2,1,0:T(8,128)(2,1)S(1)} copy-done((bf16[2,4,32,128]{3,2,1,0:T(8,128)(2,1)S(1)}, bf16[2,4,32,128]{3,2,1,0:T(8,128)(2,1)}, u32[]{:S(2)}) %copy-start.1) | copy-done | bytes 65560
  2.4 0.0 copy-start.2
  2.4 0.8 %copy-done.2 = bf16[2,2,16,256]{3,2,1,0:T(8,128)(2,1)S(1)} copy-done((bf16[2,2,16,256]{3,2,1,0:T(8,128)(2,1)S(1)}, bf16[2,2,16,256]{3,2,1,0:T(8,128)(2,1)}, u32[]{:S(2)}) %copy-start.2) | copy-done | bytes 32792
  3.1 0.0 copy-start.4
  3.1 0.0 copy-start.5
  3.1 62.5 %shard_map.109 = (f32[8,3456]{1,0:T(8,128)S(1)}, f32[2,2,16,256]{3,2,1,0:T(8,128)S(1)}, f32[2,2,16,256]{3,2,1,0:T(8,128)S(1)}, f32[1,1]{1,0:T(1,128)}) custom-call(bf16[2,2,16,256]{3,2,1,0:T(8,128)(2,1)S(1)} %copy-done.2, bf16[2,4,32,128]{3,2,1,0:T(8,128)(2,1)S(1)} %copy-done.1, f32[8,3456]{1,0:T(8,128)S(1)} %copy-done), custom_call_target="tpu_custom_call" | custom-call | tf_op jit(solution)/shard_map/pallas_call | solution.py:512
  65.6 0.0 copy-start.3
  65.6 0.6 add_convert_fusion
  66.2 0.0 copy-done.4
  66.2 0.0 copy-done.5
  66.2 0.3 copy-done.3
  66.5 0.8 %multiply_add_fusion = (f32[8,3456]{1,0:T(8,128)}, f32[8,3456]{1,0:T(8,128)}, f32[8,3456]{1,0:T(8,128)}, f32[8,3456]{1,0:T(8,128)}) fusion(f32[8,3456]{1,0:T(8,128)S(1)} %copy-done.3, f32[8,3456]{1,0:T(8,128)S(1)} %copy-done, f32[8,3456]{1,0:T(8,128)S(1)} %get-tuple-element.10, f32[8,3456]{1,0:T(8,128)S(1)} %copy-done.4, f32[8,3456]{1,0:T(8,128)S(1)} %copy-done.5), kind=kLoop, calls=%fused_computation.2 | loop fusion | flops 387072 | bytes 995328 | tf_op jit(solution)/shard_map/add | solution.py:571
Async XLA Ops:
  0.6 0.9 %copy-start = (f32[8,3456]{1,0:T(8,128)S(1)}, f32[8,3456]{1,0:T(8,128)}, u32[]{:S(2)}) copy-start(f32[8,3456]{1,0:T(8,128)} %master.1) | copy-start | bytes 331780
  1.5 0.8 %copy-start.1 = (bf16[2,4,32,128]{3,2,1,0:T(8,128)(2,1)S(1)}, bf16[2,4,32,128]{3,2,1,0:T(8,128)(2,1)}, u32[]{:S(2)}) copy-start(bf16[2,4,32,128]{3,2,1,0:T(8,128)(2,1)} %target.1) | copy-start | bytes 196612
  2.4 0.8 %copy-start.2 = (bf16[2,2,16,256]{3,2,1,0:T(8,128)(2,1)S(1)}, bf16[2,2,16,256]{3,2,1,0:T(8,128)(2,1)}, u32[]{:S(2)}) copy-start(bf16[2,2,16,256]{3,2,1,0:T(8,128)(2,1)} %latent.1) | copy-start | bytes 98308
  3.1 63.1 %copy-start.4 = (f32[8,3456]{1,0:T(8,128)S(1)}, f32[8,3456]{1,0:T(8,128)}, u32[]{:S(2)}) copy-start(f32[8,3456]{1,0:T(8,128)} %param.9) | copy-start | bytes 331780
  3.1 63.1 %copy-start.5 = (f32[8,3456]{1,0:T(8,128)S(1)}, f32[8,3456]{1,0:T(8,128)}, u32[]{:S(2)}) copy-start(f32[8,3456]{1,0:T(8,128)} %param.10) | copy-start | bytes 331780
  65.6 0.9 %copy-start.3 = (f32[8,3456]{1,0:T(8,128)S(1)}, f32[8,3456]{1,0:T(8,128)}, u32[]{:S(2)}) copy-start(f32[8,3456]{1,0:T(8,128)} %param.11) | copy-start | bytes 331780

commit v3 on v2

--- a/solution.py
+++ b/solution.py
@@ -150,6 +150,7 @@
     g_recv,
     lat_sem,
     load_sem,
+    token,
 ):
     z = lax.axis_index("tm")
     h = lax.axis_index("height")
@@ -185,26 +186,18 @@
     for j in range(1, 4):
         peers += [dev(unit(j, 0), c), dev(unit(0, j), c)]
     for dz in (-1, 0, 1):
-        for chip in (above, below):
-            for core in range(2):
-                peers.append(dev(chip, core, dz))
+        peers += [dev(above, c, dz), dev(below, c, dz)]
         if dz:
-            peers.append(dev(u, other, dz))
+            peers += [dev(u, 0, dz), dev(u, 1, dz)]
     for peer in peers:
         pl.semaphore_signal(barrier, inc=1, device_id=peer, device_id_type=MESH)
 
-    def greet(i, carry):
-        pl.semaphore_signal(barrier, inc=1, device_id=((z + i) % Z, h), device_id_type=MESH)
-        return carry
-
-    lax.fori_loop(1, Z, greet, 0)
-
     loads[0].wait()
     halves = split_halves(own_kernel[...] * SCALE)
     for a in range(3):
         pair_out[a] = jnp.where(c == 0, halves[1][a], halves[0][a])
 
-    pl.semaphore_wait(barrier, len(peers) + Z - 1)
+    pl.semaphore_wait(barrier, len(peers))
 
     sent = []
 
@@ -216,6 +209,16 @@
     def arrived(dst, sem):
         remote(dst, dst, ag_send.at[0], sem, sibling).wait_recv()
 
+    def token_out(i):
+        for step in (1 << i, -(1 << i)):
+            pl.semaphore_signal(
+                token.at[i], inc=1, device_id=dev(u, c, step), device_id_type=MESH
+            )
+
+    def token_in(i):
+        pl.semaphore_wait(token.at[i], 2)
+
+    token_out(0)
     send(pair_out, pair_in, pair_sem.at[0], pair_sem.at[1], sibling)
 
     edge = pl.ds(c, 1)
@@ -239,15 +242,14 @@
                 n += 1
         for t, dz in ((0, 1), (1, 0), (2, -1)):
             frames = pl.ds(2 * t, 2)
-            for core in range(2):
-                send(
-                    latent.at[:, edge],
-                    xe.at[frames, edge_row],
-                    x_send.at[n],
-                    x_recv.at[6 + 2 * t + c],
-                    dev(edge_to, core, dz),
-                )
-                n += 1
+            send(
+                latent.at[:, edge],
+                xe.at[frames, edge_row],
+                x_send.at[n],
+                x_recv.at[6 + 2 * t + c],
+                dev(edge_to, c, dz),
+            )
+            n += 1
 
     def send_target():
         n = 0
@@ -264,15 +266,14 @@
                     dev(u, (c + flip) % 2, dz),
                 )
                 n += 1
-            for core in range(2):
-                send(
-                    target.at[:, pl.ds(3 * c, 1)],
-                    te.at[frames, pl.ds(9 - 9 * c, 1)],
-                    t_send.at[n],
-                    t_recv.at[4 + 2 * t + c],
-                    dev(edge_to, core, dz),
-                )
-                n += 1
+            send(
+                target.at[:, pl.ds(3 * c, 1)],
+                te.at[frames, pl.ds(9 - 9 * c, 1)],
+                t_send.at[n],
+                t_recv.at[4 + 2 * t + c],
+                dev(edge_to, c, dz),
+            )
+            n += 1
 
     arrived(pair_in, pair_sem.at[1])
     for a in range(3):
@@ -298,7 +299,20 @@
         arrived(weights.at[:, index], ag_recv.at[k - 1])
         for j in far_first:
             send_unit(index, 2 + 3 * k + j, unit(0, j))
+    token_in(0)
+    token_out(1)
     send_target()
+
+    for t in range(3):
+        place = xe.at[pl.ds(2 * t, 2), edge_row]
+        sem = x_recv.at[6 + 2 * t + c]
+        arrived(place, sem)
+        send(place, place, x_send.at[8 + t], sem, sibling)
+    for t in range(2):
+        place = te.at[pl.ds(2 * t, 2), pl.ds(9 - 9 * c, 1)]
+        sem = t_recv.at[4 + 2 * t + c]
+        arrived(place, sem)
+        send(place, place, t_send.at[5 + t], sem, sibling)
 
     for load in loads[1:]:
         load.wait()
@@ -312,23 +326,24 @@
                 arrived(xe.at[pl.ds(2, 2), rows], x_recv.at[2 + other])
             else:
                 arrived(xe.at[pl.ds(2 * t, 2), rows], x_recv.at[2 * t + core])
-        for core in range(2):
-            arrived(xe.at[pl.ds(2 * t, 2), pl.ds(5 - 5 * core, 1)], x_recv.at[6 + 2 * t + core])
+        arrived(xe.at[pl.ds(2 * t, 2), pl.ds(5 - 5 * other, 1)], x_recv.at[6 + 2 * t + other])
+
+    for a in range(3):
+        xc[:, :, :, a * 256 : (a + 1) * 256] = xe[a : a + 4]
 
     @pl.when(u == 0)
     def _():
-        xe[:, 0] = jnp.zeros((6, 16, 256), BF16)
+        xc[:, 0] = jnp.zeros((4, 16, 768), BF16)
 
     @pl.when(u == 15)
     def _():
-        xe[:, 5] = jnp.zeros((6, 16, 256), BF16)
+        xc[:, 5] = jnp.zeros((4, 16, 768), BF16)
 
     @pl.when(z == 0)
     def _():
-        xe[0:2] = jnp.zeros((2, 6, 16, 256), BF16)
-
-    for a in range(3):
-        xc[:, :, :, a * 256 : (a + 1) * 256] = xe[a : a + 4]
+        xc[0:2, :, :, 0:256] = jnp.zeros((2, 6, 16, 256), BF16)
+        xc[0:1, :, :, 256:512] = jnp.zeros((1, 6, 16, 256), BF16)
+
     x_t = xe[2:4, 1:5].reshape(128, 256).astype(F32).T.astype(BF16)
 
     for t in range(2):
@@ -337,8 +352,7 @@
         else:
             for core in range(2):
                 arrived(te.at[pl.ds(2, 2), pl.ds(1 + 4 * core, 4)], t_recv.at[2 + core])
-        for core in range(2):
-            arrived(te.at[pl.ds(2 * t, 2), pl.ds(9 - 9 * core, 1)], t_recv.at[4 + 2 * t + core])
+        arrived(te.at[pl.ds(2 * t, 2), pl.ds(9 - 9 * other, 1)], t_recv.at[4 + 2 * t + other])
 
     def sort_target(f, carry):
         tf[...] = te[f].astype(F32).reshape(320, 128)
@@ -351,6 +365,8 @@
         return carry
 
     lax.fori_loop(0, 4, sort_target, 0)
+    token_in(1)
+    token_out(2)
 
     for k in (0, 3, 1, 2):
         for j in far_first:
@@ -464,6 +480,7 @@
         to = (z + i) % Z
         return remote(gsend_buf, grecv_buf.at[z], g_send.at[i], g_recv.at[z], (to, h))
 
+    token_in(2)
     order = [8] + [v for d in range(7, 0, -1) for v in (d, 16 - d)]
     for i in order:
         z_copy(i).start()
@@ -560,11 +577,12 @@
             dma((16,)),
             dma((2,)),
             dma((3,)),
+            pltpu.SemaphoreType.REGULAR((3,)),
         ],
         compiler_params=pltpu.CompilerParams(
             collective_id=0, has_side_effects=True, vmem_limit_bytes=40 * 1024 * 1024
         ),
-    )(latent, target_frames, master)
+    )(*(pltpu.with_memory_space_constraint(v, pltpu.HBM) for v in (latent, target_frames, master)))
     new_first = beta_first * first_moment + (1.0 - beta_first) * grad
     new_second = beta_second * second_moment + (1.0 - beta_second) * grad * grad
     new_master = master - learn_rate * new_first / (jnp.sqrt(new_second) + adam_eps)

time: 69.3 us -> 63.3 us (0.913)
  Pallas kernels: 62.5 us -> 58 us
  local copies, waits for them, and re-layouts: 2.77 us -> 0.28 us
  other arithmetic: 1.42 us -> 2.32 us
    pallas_call x1, Pallas kernels: 62.5 us -> 58 us  [per_device(): pl.pallas_call(kernel, out_shape=(jax.ShapeDtypeStruct(master.shape, F32)...]
    unnamed x12 -> x6, local copies, waits for them, and re-layouts: 2.77 us -> 0.28 us
    add x1, other arithmetic: 0.8 us -> 1.69 us  [per_device(): new_ema = ema_decay * ema_weights + (1.0 - ema_decay) * new_master]
where the time goes in v3:
time: 63.3 us; the launch traced here: 63 us
  Pallas kernels  58 us (92%)
  between operations  2.41 us (4%)
  other arithmetic  2.32 us (4%)
    pallas_call x1, Pallas kernels, per_device(): pl.pallas_call(kernel, out_shape=(jax.ShapeDtypeStruct(master.shape, F32)...  58 us
    add x1, other arithmetic, per_device(): new_ema = ema_decay * ema_weights + (1.0 - ema_decay) * new_master  1.69 us

profile of v3, /device:TPU:1, one launch (start us, length us, event | category | flops | bytes accessed | tf_op | source)
XLA Modules:
  0.0 63.0 jit_solution(1198260667103658135)
XLA Ops:
  0.6 0.0 copy-start.1
  0.6 0.0 copy-start.2
  0.7 58.0 %shard_map.109 = (f32[8,3456]{1,0:T(8,128)S(1)}, f32[2,2,16,256]{3,2,1,0:T(8,128)S(1)}, f32[2,2,16,256]{3,2,1,0:T(8,128)S(1)}, f32[1,1]{1,0:T(1,128)}) custom-call(bf16[2,2,16,256]{3,2,1,0:T(8,128)(2,1)} %latent.1, bf16[2,4,32,128]{3,2,1,0:T(8,128)(2,1)} %target.1, f32[8,3456]{1,0:T(8,128)} %master.1), custom_call_target="tpu_custom_call" | custom-call | tf_op jit(solution)/shard_map/pallas_call | solution.py:529
  58.7 0.0 copy-start
  58.7 0.6 add_convert_fusion
  59.3 0.0 copy-done.1
  59.3 0.0 copy-done.2
  59.3 0.3 copy-done
  59.6 1.7 %multiply_add_fusion = (f32[8,3456]{1,0:T(8,128)}, f32[8,3456]{1,0:T(8,128)}, f32[8,3456]{1,0:T(8,128)}, f32[8,3456]{1,0:T(8,128)}) fusion(f32[8,3456]{1,0:T(8,128)S(1)} %copy-done.1, f32[8,3456]{1,0:T(8,128)S(1)} %copy-done, f32[8,3456]{1,0:T(8,128)S(1)} %get-tuple-element.10, f32[8,3456]{1,0:T(8,128)S(1)} %copy-done.2, f32[8,3456]{1,0:T(8,128)} %param.10), kind=kLoop, calls=%fused_computation.2 | loop fusion | flops 387072 | bytes 995328 | tf_op jit(solution)/shard_map/add | solution.py:589
Async XLA Ops:
  0.6 58.7 %copy-start.1 = (f32[8,3456]{1,0:T(8,128)S(1)}, f32[8,3456]{1,0:T(8,128)}, u32[]{:S(2)}) copy-start(f32[8,3456]{1,0:T(8,128)} %param.11) | copy-start | bytes 331780
  0.6 58.7 %copy-start.2 = (f32[8,3456]{1,0:T(8,128)S(1)}, f32[8,3456]{1,0:T(8,128)}, u32[]{:S(2)}) copy-start(f32[8,3456]{1,0:T(8,128)} %param.9) | copy-start | bytes 331780
  58.7 0.9 %copy-start = (f32[8,3456]{1,0:T(8,128)S(1)}, f32[8,3456]{1,0:T(8,128)}, u32[]{:S(2)}) copy-start(f32[8,3456]{1,0:T(8,128)} %master.1) | copy-start | bytes 331780

commit v4 on v3

v4 whole, which is shorter than its diff:
```python
import math

import jax
import jax.numpy as jnp
from jax import lax
from jax.experimental import pallas as pl
from jax.experimental.pallas import tpu as pltpu
from jax.sharding import PartitionSpec as P

learn_rate = 0.3
beta_first = 0.9
beta_second = 0.99
ema_decay = 0.9
adam_eps = 1e-08

MESH = pl.DeviceIdType.MESH
F32 = jnp.float32
BF16 = jnp.bfloat16
SCALE = 1.0 / math.sqrt(27 * 256)
BLOCKS = 7
Z = 16


def group_of(shape):
    return lax.broadcasted_iota(jnp.int32, shape, len(shape) - 1) // 32


def turn(v, groups):
    if isinstance(groups, int) and groups % 4 == 0:
        return v
    return pltpu.roll(v, (groups + 8) % 4 * 32, axis=v.ndim - 1)


def by_group(parts):
    group = group_of(parts[0].shape)
    v = parts[3]
    for i in (2, 1, 0):
        v = jnp.where(group == i, parts[i], v)
    return v


def col_of(shape):
    return lax.broadcasted_iota(jnp.int32, shape, 0) % 16


def from_left(v):
    return jnp.where(col_of(v.shape) == 0, 0.0, pltpu.roll(v, 1, axis=0))


def from_right(v):
    return jnp.where(col_of(v.shape) == 15, 0.0, pltpu.roll(v, v.shape[0] - 1, axis=0))


def quarter_of(m, quarter):
    def tap(a, n, group):
        t = 9 * a + n
        return turn(m[:, t * 128 : (t + 1) * 128], group - quarter)

    blocks = [by_group([tap(a, 4 * k + g, g) for g in range(4)]) for k in range(2) for a in range(3)]
    return blocks + [by_group([tap(g, 8, g) for g in range(3)] + [jnp.zeros((8, 128), F32)])]


def outputs_of(z):
    u = []
    for b in range(3):
        z0, z1, z2 = (turn(z[(3 * b + e) // 4], -((3 * b + e) % 4)) for e in range(3))
        u.append((from_left(z0) + z1 + z2, z0 + z1 + from_right(z2)))
    out = ([], [])
    for j in range(2):
        common = u[0][j][0:80] + u[2][j][16:96]
        out[0].append(common + u[1][j][16:96])
        out[1].append(common + u[1][j][0:80])
    return out


def folded(g):
    slots = []
    for b in range(3):
        v = []
        for j in range(2):
            g0, g1 = g[0][j], g[1][j]
            v.append((g1[16:80] + g0[16:80], g0[0:64] + g1[16:80], g1[0:64] + g0[0:64])[b])
        slots += [v[1] + from_right(v[0]), v[0] + v[1], from_left(v[1]) + v[0]]
    zero = jnp.zeros((64, 128), F32)
    slots += [zero] * 3
    return [by_group([turn(slots[4 * k + g], g) if 4 * k + g < 9 else zero for g in range(4)]) for k in range(3)]


def remote(src, dst, send_sem, recv_sem, device):
    return pltpu.make_async_remote_copy(
        src_ref=src,
        dst_ref=dst,
        send_sem=send_sem,
        recv_sem=recv_sem,
        device_id=device,
        device_id_type=MESH,
    )


def kernel(
    latent,
    target,
    master,
    out_grad,
    out_own,
    out_other,
    out_loss,
    own_kernel,
    pair_out,
    pair_in,
    weights,
    xe,
    xc,
    te,
    tf,
    tp,
    zs,
    hs,
    h9,
    dw,
    got_b,
    part_b,
    got_a,
    swap_out,
    swap_in,
    zsend_buf,
    zrecv_buf,
    gsend_buf,
    grecv_buf,
    lat_out,
    pair_sem,
    ag_send,
    ag_recv,
    x_send,
    x_recv,
    t_send,
    t_recv,
    rb_send,
    rb_recv,
    ra_send,
    ra_recv,
    swap_sem,
    z_send,
    z_recv,
    g_send,
    g_recv,
    lat_sem,
    load_sem,
    token,
):
    z = lax.axis_index("tm")
    h = lax.axis_index("height")
    c = h % 2
    u = h // 2
    s = z % 2
    partner = 1 - 2 * s
    quarter = 2 * s + c
    other = 1 - c
    sa, sb = 4 - 3 * c, 1 + 3 * c
    pa = jnp.where(c == 0, u // 4, u % 4)
    pb = jnp.where(c == 0, u % 4, u // 4)

    def unit(da, db):
        return ((pa + da) % 4) * sa + ((pb + db) % 4) * sb

    def dev(chip, core, dz=0):
        return ((z + dz + Z) % Z, chip * 2 + core)

    sibling = dev(u, other)
    above, below = (u + 15) % 16, (u + 1) % 16
    own_rows = pl.ds(1 + 2 * c, 2)
    t_rows = pl.ds(1 + 4 * c, 4)
    own_x, own_t = pl.ds(2 + 2 * s, 2), pl.ds(2 * s, 2)

    loads = [
        pltpu.make_async_copy(src, dst, load_sem.at[i])
        for i, (src, dst) in enumerate(
            ((master, own_kernel), (latent, xe.at[own_x, own_rows]), (target, te.at[own_t, t_rows]))
        )
    ]
    for load in loads:
        load.start()

    barrier = pltpu.get_barrier_semaphore()
    peers = [sibling]
    for j in range(1, 4):
        peers += [dev(unit(j, 0), c), dev(unit(0, j), c)]
    for dz in (-2, -1, 0, 1, 2):
        peers += [dev(above, c, dz), dev(below, c, dz)]
        if dz:
            peers += [dev(u, 0, dz), dev(u, 1, dz)]
    for peer in peers:
        pl.semaphore_signal(barrier, inc=1, device_id=peer, device_id_type=MESH)

    loads[0].wait()
    scaled = own_kernel[...] * SCALE
    for i, block in enumerate(quarter_of(scaled, 2 * s + other)):
        pair_out[i] = block
    mine = quarter_of(scaled, quarter)

    pl.semaphore_wait(barrier, len(peers))

    sent = []

    def send(*args):
        copy = remote(*args)
        copy.start()
        sent.append(copy)

    def arrived(dst, sem):
        remote(dst, dst, ag_send.at[0], sem, sibling).wait_recv()

    def token_out(i):
        for step in (1 << i, -(1 << i)):
            pl.semaphore_signal(
                token.at[i], inc=1, device_id=dev(u, c, step), device_id_type=MESH
            )

    def token_in(i):
        pl.semaphore_wait(token.at[i], 2)

    token_out(0)
    send(pair_out, pair_in, pair_sem.at[0], pair_sem.at[1], sibling)

    edge = pl.ds(c, 1)
    edge_to = jnp.where(c == 0, above, below)
    edge_row = pl.ds(5 - 5 * c, 1)
    beside = 2 * s - 1
    routes = ((0, 1 + s), (partner, 1 + s), (beside, 3 - 3 * s), (2 * beside, 3 - 3 * s))

    def send_latent():
        n = 0
        for i, (dz, t) in enumerate(routes):
            frames = pl.ds(2 * t, 2)
            for flip in range(2):
                if i or flip:
                    send(
                        latent,
                        xe.at[frames, own_rows],
                        x_send.at[n],
                        x_recv.at[2 * t + c],
                        dev(u, (c + flip) % 2, dz),
                    )
                    n += 1
        for dz, t in routes:
            send(
                latent.at[:, edge],
                xe.at[pl.ds(2 * t, 2), edge_row],
                x_send.at[n],
                x_recv.at[8 + 2 * t + c],
                dev(edge_to, c, dz),
            )
            n += 1

    def target_copies(first, steps, slot):
        copies = []
        frames = pl.ds(2 * slot, 2)
        for dz in steps:
            for flip in range(2):
                if flip or not isinstance(dz, int) or dz:
                    copies.append(
                        remote(
                            target,
                            te.at[frames, t_rows],
                            t_send.at[first + len(copies)],
                            t_recv.at[2 * slot + c],
                            dev(u, (c + flip) % 2, dz),
                        )
                    )
            copies.append(
                remote(
                    target.at[:, pl.ds(3 * c, 1)],
                    te.at[frames, pl.ds(9 - 9 * c, 1)],
                    t_send.at[first + len(copies)],
                    t_recv.at[6 + 2 * slot + c],
                    dev(edge_to, c, dz),
                )
            )
        return copies

    def send_target():
        for copy in target_copies(0, (0, partner), s):
            copy.start()
            sent.append(copy)

        @pl.when(s == 0)
        def _():
            for copy in target_copies(5, (-1, -2), 2):
                copy.start()

    send_latent()
    send_target()

    arrived(pair_in, pair_sem.at[1])
    for i in range(BLOCKS):
        theirs = pair_in[i]
        rows = jnp.concatenate(
            [jnp.where(c == 0, mine[i], theirs), jnp.where(c == 0, theirs, mine[i])], axis=0
        )
        weights[i, u] = rows.astype(BF16)

    def send_unit(index, sem, to):
        place = weights.at[:, index]
        send(place, place, ag_send.at[sem], ag_recv.at[sem], dev(to, c))

    far_first = (2, 1, 3)
    for j in far_first:
        send_unit(u, j - 1, unit(j, 0))
    for j in far_first:
        send_unit(u, 2 + j, unit(0, j))
    for k in (1, 3, 2):
        index = unit(4 - k, 0)
        arrived(weights.at[:, index], ag_recv.at[k - 1])
        for j in far_first:
            send_unit(index, 2 + 3 * k + j, unit(0, j))
    token_in(0)
    token_out(1)

    for t in range(4):
        place = xe.at[pl.ds(2 * t, 2), edge_row]
        arrived(place, x_recv.at[8 + 2 * t + c])
        send(place, place, x_send.at[11 + t], x_recv.at[8 + 2 * t + c], sibling)
    for t in range(3):
        place = te.at[pl.ds(2 * t, 2), pl.ds(9 - 9 * c, 1)]
        arrived(place, t_recv.at[6 + 2 * t + c])
        send(place, place, t_send.at[11 + t], t_recv.at[6 + 2 * t + c], sibling)

    for load in loads[1:]:
        load.wait()
    for t, core in ((0, 0), (0, 1), (3, 0), (3, 1), (2 - s, 0), (2 - s, 1), (1 + s, other)):
        arrived(xe.at[pl.ds(2 * t, 2), pl.ds(1 + 2 * core, 2)], x_recv.at[2 * t + core])
    for t in range(4):
        arrived(xe.at[pl.ds(2 * t, 2), pl.ds(5 - 5 * other, 1)], x_recv.at[8 + 2 * t + other])

    for a in range(3):
        xc[:, :, :, a * 256 : (a + 1) * 256] = xe[a : a + 6]

    @pl.when(u == 0)
    def _():
        xc[:, 0] = jnp.zeros((6, 16, 768), BF16)

    @pl.when(u == 15)
    def _():
        xc[:, 5] = jnp.zeros((6, 16, 768), BF16)

    @pl.when(z < 2)
    def _():
        xc[0:2, :, :, 0:256] = jnp.zeros((2, 6, 16, 256), BF16)
        xc[0:1, :, :, 256:512] = jnp.zeros((1, 6, 16, 256), BF16)

    x_t = xe[2:6, 1:5].reshape(256, 256).astype(F32).T.astype(BF16)

    for t, core in ((2, 0), (2, 1), (1 - s, 0), (1 - s, 1), (s, other)):
        arrived(te.at[pl.ds(2 * t, 2), pl.ds(1 + 4 * core, 4)], t_recv.at[2 * t + core])
    for t in range(3):
        arrived(te.at[pl.ds(2 * t, 2), pl.ds(9 - 9 * other, 1)], t_recv.at[6 + 2 * t + other])

    def sort_target(f, carry):
        tf[...] = te[f].astype(F32).reshape(320, 128)
        for i in range(2):
            for j in range(2):
                for r in range(5):
                    row = 2 * r + 1 - i
                    v = tf[pl.ds(row * 32 + j, 16, stride=2), :]
                    tp[f, i, j, r * 16 : (r + 1) * 16, :] = turn(v, -quarter)
        return carry

    lax.fori_loop(0, 6, sort_target, 0)
    token_in(1)
    token_out(2)

    for k in (0, 3, 1, 2):
        for j in far_first:
            arrived(weights.at[:, unit(4 - k, 4 - j)], ag_recv.at[2 + 3 * k + j])

    ninth = weights[6].reshape(256, 128).astype(F32)
    by_slot = jnp.concatenate(
        [
            weights[0:3].reshape(768, 128),
            weights[3:6].reshape(768, 128),
            jnp.concatenate([turn(ninth, -a).astype(BF16) for a in range(3)], axis=0),
        ],
        axis=1,
    )
    zs[...] = jnp.dot(
        xc[...].reshape(576, 768), by_slot, preferred_element_type=F32
    ).reshape(6, 96, 384)

    def frame(f, loss):
        out = outputs_of([zs[f, :, k * 128 : (k + 1) * 128] for k in range(3)])
        row = lax.broadcasted_iota(jnp.int32, (80, 128), 0)
        keep = jnp.logical_or(f < 4, z < Z - 2)
        keep0 = jnp.logical_and(keep, jnp.logical_or(row < 64, u < 15))
        keep1 = jnp.logical_and(keep, jnp.logical_or(row >= 16, u > 0))
        own = jnp.where(f < 4, 1.0, 0.0)
        g = ([], [])
        for i in range(2):
            for j in range(2):
                misfit = out[i][j] - tp[f, i, j]
                counted = misfit[16 * i : 16 * i + 64]
                loss = loss + own * jnp.sum(counted * counted, axis=0, keepdims=True)
                rounded = misfit.astype(BF16).astype(F32)
                g[i].append(jnp.where((keep0, keep1)[i], rounded, 0.0))
        blocks = folded(g)
        for k in range(2):
            hs[f, :, k * 128 : (k + 1) * 128] = blocks[k].astype(BF16)
        h9[f] = blocks[2]
        return loss

    chunks = ((0, 2), (2, 2), (4, 3))

    def kernel_gradient(i):
        a = 2 - i
        first, n = chunks[i]
        part = jnp.dot(x_t, hs[2 - a : 6 - a].reshape(256, 256), preferred_element_type=F32)
        parts = [part[:, 0:128], part[:, 128:256]]
        if n == 3:
            parts.append(jnp.dot(x_t, ninths(), preferred_element_type=F32) + loss)
        for v in range(16):
            in_b = jnp.where(c == 0, v % 4, v // 4)
            in_a = jnp.where(c == 0, v // 4, v % 4)
            for k in range(n):
                dw[first + k, in_b, in_a] = parts[k][16 * v : 16 * v + 16].astype(BF16)
        for j in far_first:
            sem = 3 * i + j - 1
            send(
                dw.at[pl.ds(first, n), (pb + j) % 4],
                got_b.at[pl.ds(first, n), j - 1],
                rb_send.at[sem],
                rb_recv.at[sem],
                dev(unit(0, j), c),
            )

    def ninths():
        v = h9[2:6].reshape(256, 128)
        for a in (1, 2):
            v = v + turn(h9[2 - a : 6 - a].reshape(256, 128), a)
        return v.astype(BF16)

    loss = lax.fori_loop(0, 4, frame, jnp.zeros((1, 128), F32))
    loss = jnp.where(group_of((1, 128)) == 3, turn(loss, 3), 0.0)
    kernel_gradient(0)
    for i in (1, 2):
        frame(3 + i, jnp.zeros((1, 128), F32))
        kernel_gradient(i)

    over_last = (((1,), (1,)), ((), ()))
    lat = lax.dot_general(
        ninths(), weights[6].reshape(256, 128), over_last, preferred_element_type=F32
    )
    for a in range(3):
        both = jnp.concatenate(
            [weights[a].reshape(256, 128), weights[3 + a].reshape(256, 128)], axis=1
        )
        lat = lat + lax.dot_general(
            hs[2 - a : 6 - a].reshape(256, 256), both, over_last, preferred_element_type=F32
        )
    lat = lat.reshape(4, 4, 16, 256)
    for i in range(2):
        for core in range(2):
            lat_out[i, core] = lat[2 * i : 2 * i + 2, 2 * core : 2 * core + 2]
    out_own[...] = lat_out[s, c]
    for i, (dz, side, core) in enumerate(((0, s, other), (partner, 1 - s, c), (partner, 1 - s, other))):
        send(
            lat_out.at[side, core],
            out_other.at[i],
            lat_sem.at[i],
            lat_sem.at[3 + i],
            dev(u, core, dz),
        )

    kept = {}

    def axis_a(i):
        first, n = chunks[i]
        part = pl.ds(first, n)
        for j in range(1, 4):
            arrived(got_b.at[part, j - 1], rb_recv.at[3 * i + j - 1])
        for k in far_first + (0,):
            at = (pa + k) % 4
            rows = dw[part, pb, at].astype(F32)
            for j in range(3):
                rows = rows + got_b[part, j, at].astype(F32)
            part_b[part, k] = rows.astype(BF16)
            if k:
                sem = 3 * i + k - 1
                send(
                    part_b.at[part, k],
                    got_a.at[part, k - 1],
                    ra_send.at[sem],
                    ra_recv.at[sem],
                    dev(unit(k, 0), c),
                )

    def swap(i):
        first, n = chunks[i]
        part = pl.ds(first, n)
        rows = part_b[part, 0].astype(F32)
        for j in range(1, 4):
            arrived(got_a.at[part, j - 1], ra_recv.at[3 * i + j - 1])
            rows = rows + got_a[part, j - 1].astype(F32)
        swap_out[part] = jnp.where(c == 0, rows[:, 8:16], rows[:, 0:8])
        kept[i] = jnp.where(c == 0, rows[:, 0:8], rows[:, 8:16])
        send(swap_out.at[part], swap_in.at[part], swap_sem.at[i], swap_sem.at[3 + i], sibling)

    def z_block(p):
        return remote(
            zsend_buf.at[p], zrecv_buf.at[z // 2], z_send.at[p], z_recv.at[z // 2], (2 * p + s, h)
        )

    def along_z(i):
        first, n = chunks[i]
        part = pl.ds(first, n)
        arrived(swap_in.at[part], swap_sem.at[3 + i])
        theirs = swap_in[part]
        zsend_buf[part] = jnp.concatenate(
            [jnp.where(c == 0, kept[i], theirs), jnp.where(c == 0, theirs, kept[i])], axis=1
        ).astype(BF16)
        for p in range(first, first + n):

            @pl.when(z // 2 != p)
            def _():
                z_block(p).start()

    axis_a(0)
    axis_a(1)
    swap(0)
    axis_a(2)
    token_in(2)
    along_z(0)
    swap(1)
    along_z(1)
    swap(2)
    along_z(2)

    def g_copy(i):
        to = (z + i) % Z
        return remote(gsend_buf, grecv_buf.at[z], g_send.at[i], g_recv.at[z], (to, h))

    order = [8] + [v for d in range(7, 0, -1) for v in (d, 16 - d)]

    @pl.when(z < 14)
    def _():
        acc = zsend_buf[z // 2].astype(F32)
        for i in (1, 7, 2, 6, 3, 5, 4):
            source = (z // 2 + i) % 8
            arrived(zrecv_buf.at[source], z_recv.at[source])
            acc = acc + zrecv_buf[source].astype(F32)
        gsend_buf[...] = acc.astype(BF16)
        for i in order:
            g_copy(i).start()
        grecv_buf[z] = gsend_buf[...]

    for i in range(3):
        arrived(out_other.at[i], lat_sem.at[3 + i])
    for copy in sent:
        copy.wait_send()
    @pl.when(s == 0)
    def _():
        for copy in target_copies(5, (-1, -2), 2):
            copy.wait_send()

    for p in range(BLOCKS):

        @pl.when(z // 2 != p)
        def _():
            z_block(p).wait_send()

    def grad_tap(t, pieces, group):
        out_grad[:, t * 128 : (t + 1) * 128] = SCALE * by_group(
            [turn(pieces[q], q - group) for q in range(4)]
        )

    for p in range(BLOCKS):
        pieces = []
        for i in range(2):
            at = 2 * p + i

            @pl.when(z != at)
            def _():
                arrived(grecv_buf.at[at], g_recv.at[at])

            both = grecv_buf[at].astype(F32)
            pieces += [both[0:8], both[8:16]]
        for g in range(4):
            if p < 6:
                grad_tap(9 * (2 - p // 2) + 4 * (p % 2) + g, pieces, g)
            elif g < 3:
                grad_tap(9 * g + 8, pieces, g)
    whole = (pieces[0] + pieces[1] + pieces[2] + pieces[3])[0:1]
    whole = jnp.where(group_of((1, 128)) == 3, whole, 0.0)
    out_loss[0, 0] = jnp.sum(whole) * (1.0 / 16777216)

    @pl.when(z < 14)
    def _():
        for i in order:
            g_copy(i).wait_send()


def per_device(latent, target_frames, master, first_moment, second_moment, ema_weights):
    vmem = pl.BlockSpec(memory_space=pltpu.VMEM)
    hbm = pl.BlockSpec(memory_space=pltpu.HBM)
    dma = pltpu.SemaphoreType.DMA
    quarter_grad = jax.ShapeDtypeStruct(latent.shape, F32)
    grad, own, other, loss = pl.pallas_call(
        kernel,
        out_shape=(
            jax.ShapeDtypeStruct(master.shape, F32),
            quarter_grad,
            jax.ShapeDtypeStruct((3, *latent.shape), F32),
            jax.ShapeDtypeStruct((1, 1), F32),
        ),
        in_specs=[hbm, hbm, hbm],
        out_specs=(vmem, vmem, vmem, pl.BlockSpec(memory_space=pltpu.SMEM)),
        scratch_shapes=[
            pltpu.VMEM((8, 3456), F32),
            pltpu.VMEM((BLOCKS, 8, 128), F32),
            pltpu.VMEM((BLOCKS, 8, 128), F32),
            pltpu.VMEM((BLOCKS, 16, 16, 128), BF16),
            pltpu.VMEM((8, 6, 16, 256), BF16),
            pltpu.VMEM((6, 6, 16, 768), BF16),
            pltpu.VMEM((6, 10, 32, 128), BF16),
            pltpu.VMEM((320, 128), F32),
            pltpu.VMEM((6, 2, 2, 80, 128), F32),
            pltpu.VMEM((6, 96, 384), F32),
            pltpu.VMEM((6, 64, 256), BF16),
            pltpu.VMEM((6, 64, 128), F32),
            pltpu.VMEM((BLOCKS, 4, 4, 16, 128), BF16),
            pltpu.VMEM((BLOCKS, 3, 4, 16, 128), BF16),
            pltpu.VMEM((BLOCKS, 4, 16, 128), BF16),
            pltpu.VMEM((BLOCKS, 3, 16, 128), BF16),
            pltpu.VMEM((BLOCKS, 8, 128), F32),
            pltpu.VMEM((BLOCKS, 8, 128), F32),
            pltpu.VMEM((BLOCKS, 16, 128), BF16),
            pltpu.VMEM((8, 16, 128), BF16),
            pltpu.VMEM((16, 128), BF16),
            pltpu.VMEM((16, 16, 128), BF16),
            pltpu.VMEM((2, 2, 2, 2, 16, 256), F32),
            dma((2,)),
            dma((15,)),
            dma((15,)),
            dma((15,)),
            dma((16,)),
            dma((14,)),
            dma((12,)),
            dma((9,)),
            dma((9,)),
            dma((9,)),
            dma((9,)),
            dma((6,)),
            dma((8,)),
            dma((8,)),
            dma((16,)),
            dma((16,)),
            dma((6,)),
            dma((3,)),
            pltpu.SemaphoreType.REGULAR((3,)),
        ],
        compiler_params=pltpu.CompilerParams(
            collective_id=0, has_side_effects=True, vmem_limit_bytes=40 * 1024 * 1024
        ),
    )(*(pltpu.with_memory_space_constraint(v, pltpu.HBM) for v in (latent, target_frames, master)))
    new_first = beta_first * first_moment + (1.0 - beta_first) * grad
    new_second = beta_second * second_moment + (1.0 - beta_second) * grad * grad
    new_master = master - learn_rate * new_first / (jnp.sqrt(new_second) + adam_eps)
    new_ema = ema_decay * ema_weights + (1.0 - ema_decay) * new_master
    latent_grad = (own + other[0] + other[1] + other[2]).astype(BF16)
    return (new_master, new_first, new_second, new_ema, latent_grad, loss.reshape(()))


def solution(mesh):
    placed = (
        P("tm", "height", None, None),
        P("tm", "height", None, None),
        P("height", None),
        P("height", None),
        P("height", None),
        P("height", None),
    )
    return jax.shard_map(
        per_device,
        mesh=mesh,
        in_specs=placed,
        out_specs=(
            P("height", None),
            P("height", None),
            P("height", None),
            P("height", None),
            P("tm", "height", None, None),
            P(),
        ),
        check_vma=False,
    )
```

time: 63.3 us -> 63.2 us (level)
  Pallas kernels: 58 us -> 58.9 us
  other arithmetic: 2.32 us -> 1.43 us
    pallas_call x1, Pallas kernels: 58 us -> 58.9 us  [per_device(): pl.pallas_call(kernel, out_shape=(jax.ShapeDtypeStruct(master.shape, F32)...]
    add x1, other arithmetic: 1.69 us -> 0.8 us  [per_device(): new_ema = ema_decay * ema_weights + (1.0 - ema_decay) * new_master]
where the time goes in v4:
time: 63.2 us; the launch traced here: 63 us
  Pallas kernels  58.9 us (93%)
  between operations  2.36 us (4%)
  other arithmetic  1.43 us (2%)
    pallas_call x1, Pallas kernels, per_device(): pl.pallas_call(kernel, out_shape=(jax.ShapeDtypeStruct(master.shape, F32)...  58.9 us

profile of v4, /device:TPU:1, one launch (start us, length us, event | category | flops | bytes accessed | tf_op | source)
XLA Modules:
  0.0 63.0 jit_solution(17275200794874812295)
XLA Ops:
  0.6 0.0 copy-start.2
  0.6 0.0 copy-start.3
  0.7 58.9 %shard_map.109 = (f32[8,3456]{1,0:T(8,128)S(1)}, f32[2,2,16,256]{3,2,1,0:T(8,128)S(1)}, f32[3,2,2,16,256]{4,3,2,1,0:T(8,128)S(1)}, f32[1,1]{1,0:T(1,128)}) custom-call(bf16[2,2,16,256]{3,2,1,0:T(8,128)(2,1)} %latent.1, bf16[2,4,32,128]{3,2,1,0:T(8,128)(2,1)} %target.1, f32[8,3456]{1,0:T(8,128)} %master.1), custom_call_target="tpu_custom_call" | custom-call | tf_op jit(solution)/shard_map/pallas_call | solution.py:605
  59.6 0.0 copy-start
  59.6 0.0 copy-start.1
  59.6 0.6 %fusion.1 = bf16[2,2,16,256]{3,2,1,0:T(8,128)(2,1)} fusion(f32[2,2,16,256]{3,2,1,0:T(8,128)S(1)} %get-tuple-element.11, f32[3,2,2,16,256]{4,3,2,1,0:T(8,128)S(1)} %get-tuple-element.12), kind=kLoop, calls=%fused_computation.6 | loop fusion | flops 65536 | bytes 294912 | tf_op jit(solution)/shard_map/convert_element_type | solution.py:667
  60.2 0.0 copy-done.2
  60.2 0.0 copy-done.3
  60.2 0.2 copy-done
  60.5 0.1 copy-done.1
  60.5 0.8 %multiply_add_fusion = (f32[8,3456]{1,0:T(8,128)}, f32[8,3456]{1,0:T(8,128)}, f32[8,3456]{1,0:T(8,128)}, f32[8,3456]{1,0:T(8,128)}) fusion(f32[8,3456]{1,0:T(8,128)S(1)} %copy-done.1, f32[8,3456]{1,0:T(8,128)S(1)} %copy-done, f32[8,3456]{1,0:T(8,128)S(1)} %get-tuple-element.10, f32[8,3456]{1,0:T(8,128)S(1)} %copy-done.2, f32[8,3456]{1,0:T(8,128)S(1)} %copy-done.3), kind=kLoop, calls=%fused_computation.2 | loop fusion | flops 387072 | bytes 995328 | tf_op jit(solution)/shard_map/add | solution.py:666
Async XLA Ops:
  0.6 59.6 %copy-start.2 = (f32[8,3456]{1,0:T(8,128)S(1)}, f32[8,3456]{1,0:T(8,128)}, u32[]{:S(2)}) copy-start(f32[8,3456]{1,0:T(8,128)} %param.9) | copy-start | bytes 331780
  0.6 59.6 %copy-start.3 = (f32[8,3456]{1,0:T(8,128)S(1)}, f32[8,3456]{1,0:T(8,128)}, u32[]{:S(2)}) copy-start(f32[8,3456]{1,0:T(8,128)} %param.10) | copy-start | bytes 331780
  59.6 0.9 %copy-start = (f32[8,3456]{1,0:T(8,128)S(1)}, f32[8,3456]{1,0:T(8,128)}, u32[]{:S(2)}) copy-start(f32[8,3456]{1,0:T(8,128)} %master.1) | copy-start | bytes 331780
  59.6 1.0 %copy-start.1 = (f32[8,3456]{1,0:T(8,128)S(1)}, f32[8,3456]{1,0:T(8,128)}, u32[]{:S(2)}) copy-start(f32[8,3456]{1,0:T(8,128)} %param.11) | copy-start | bytes 331780

commit v5 on v4

--- a/solution.py
+++ b/solution.py
@@ -113,6 +113,10 @@
     xc,
     te,
     tf,
+    tpack,
+    epack,
+    tq,
+    eq,
     tp,
     zs,
     hs,
@@ -169,13 +173,12 @@
     sibling = dev(u, other)
     above, below = (u + 15) % 16, (u + 1) % 16
     own_rows = pl.ds(1 + 2 * c, 2)
-    t_rows = pl.ds(1 + 4 * c, 4)
-    own_x, own_t = pl.ds(2 + 2 * s, 2), pl.ds(2 * s, 2)
+    own_x = pl.ds(2 + 2 * s, 2)
 
     loads = [
         pltpu.make_async_copy(src, dst, load_sem.at[i])
         for i, (src, dst) in enumerate(
-            ((master, own_kernel), (latent, xe.at[own_x, own_rows]), (target, te.at[own_t, t_rows]))
+            ((master, own_kernel), (latent, xe.at[own_x, own_rows]), (target, te))
         )
     ]
     for load in loads:
@@ -231,17 +234,14 @@
     def send_latent():
         n = 0
         for i, (dz, t) in enumerate(routes):
-            frames = pl.ds(2 * t, 2)
-            for flip in range(2):
-                if i or flip:
-                    send(
-                        latent,
-                        xe.at[frames, own_rows],
-                        x_send.at[n],
-                        x_recv.at[2 * t + c],
-                        dev(u, (c + flip) % 2, dz),
-                    )
-                    n += 1
+            send(
+                latent,
+                xe.at[pl.ds(2 * t, 2), own_rows],
+                x_send.at[n],
+                x_recv.at[2 * t + c],
+                dev(u, c if i else other, dz),
+            )
+            n += 1
         for dz, t in routes:
             send(
                 latent.at[:, edge],
@@ -252,44 +252,52 @@
             )
             n += 1
 
+    def pack_target():
+        tf[...] = te[...].astype(F32).reshape(256, 128)
+        edges = []
+        for f in range(2):
+            for j in range(2):
+                rows = [tf[pl.ds((4 * f + r) * 32 + j, 16, stride=2), :] for r in range(4)]
+                for q in range(4):
+                    tpack[q, f, j] = by_group([turn(rows[r], r - q) for r in range(4)]).astype(BF16)
+                edges.append(jnp.where(c == 0, rows[0], rows[3]))
+        for q in range(4):
+            epack[q] = by_group([turn(edges[g], g - q) for g in range(4)]).astype(BF16)
+        tq[s, c] = tpack[quarter]
+
     def target_copies(first, steps, slot):
         copies = []
-        frames = pl.ds(2 * slot, 2)
-        for dz in steps:
-            for flip in range(2):
-                if flip or not isinstance(dz, int) or dz:
-                    copies.append(
-                        remote(
-                            target,
-                            te.at[frames, t_rows],
-                            t_send.at[first + len(copies)],
-                            t_recv.at[2 * slot + c],
-                            dev(u, (c + flip) % 2, dz),
-                        )
-                    )
-            copies.append(
-                remote(
-                    target.at[:, pl.ds(3 * c, 1)],
-                    te.at[frames, pl.ds(9 - 9 * c, 1)],
-                    t_send.at[first + len(copies)],
-                    t_recv.at[6 + 2 * slot + c],
-                    dev(edge_to, c, dz),
-                )
+
+        def add(src, dst, recv_sem, device):
+            copies.append(remote(src, dst, t_send.at[first + len(copies)], recv_sem, device))
+
+        for dz, side in steps:
+            near = isinstance(dz, int) and dz == 0
+            for core in (other,) if near else (c, other):
+                add(tpack.at[2 * side + core], tq.at[slot, c], t_recv.at[2 * slot + c], dev(u, core, dz))
+            add(
+                epack.at[pl.ds(2 * side, 2)],
+                eq.at[slot, c],
+                t_recv.at[6 + 2 * slot + c],
+                dev(edge_to, c, dz),
             )
         return copies
 
+    def late_copies():
+        return target_copies(5, ((-1, 1), (-2, 0)), 2)
+
     def send_target():
-        for copy in target_copies(0, (0, partner), s):
+        for copy in target_copies(0, ((0, s), (partner, 1 - s)), s):
             copy.start()
             sent.append(copy)
 
         @pl.when(s == 0)
         def _():
-            for copy in target_copies(5, (-1, -2), 2):
+            for copy in late_copies():
                 copy.start()
 
-    send_latent()
-    send_target()
+    loads[2].wait()
+    pack_target()
 
     arrived(pair_in, pair_sem.at[1])
     for i in range(BLOCKS):
@@ -308,6 +316,8 @@
         send_unit(u, j - 1, unit(j, 0))
     for j in far_first:
         send_unit(u, 2 + j, unit(0, j))
+    send_latent()
+    send_target()
     for k in (1, 3, 2):
         index = unit(4 - k, 0)
         arrived(weights.at[:, index], ag_recv.at[k - 1])
@@ -316,20 +326,23 @@
     token_in(0)
     token_out(1)
 
+    def hand_on(place, send_sem, recv_sem):
+        arrived(place, recv_sem)
+        send(place, place, send_sem, recv_sem, sibling)
+
+    for n, t in enumerate((2 - s, 3, 0)):
+        hand_on(xe.at[pl.ds(2 * t, 2), own_rows], x_send.at[12 + n], x_recv.at[2 * t + c])
     for t in range(4):
-        place = xe.at[pl.ds(2 * t, 2), edge_row]
-        arrived(place, x_recv.at[8 + 2 * t + c])
-        send(place, place, x_send.at[11 + t], x_recv.at[8 + 2 * t + c], sibling)
+        hand_on(xe.at[pl.ds(2 * t, 2), edge_row], x_send.at[8 + t], x_recv.at[8 + 2 * t + c])
     for t in range(3):
-        place = te.at[pl.ds(2 * t, 2), pl.ds(9 - 9 * c, 1)]
-        arrived(place, t_recv.at[6 + 2 * t + c])
-        send(place, place, t_send.at[11 + t], t_recv.at[6 + 2 * t + c], sibling)
-
-    for load in loads[1:]:
-        load.wait()
-    for t, core in ((0, 0), (0, 1), (3, 0), (3, 1), (2 - s, 0), (2 - s, 1), (1 + s, other)):
-        arrived(xe.at[pl.ds(2 * t, 2), pl.ds(1 + 2 * core, 2)], x_recv.at[2 * t + core])
+        recv_sem = t_recv.at[6 + 2 * t + c]
+        arrived(eq.at[t, c], recv_sem)
+        place = eq.at[t, c, other]
+        send(place, place, t_send.at[11 + t], recv_sem, sibling)
+
+    loads[1].wait()
     for t in range(4):
+        arrived(xe.at[pl.ds(2 * t, 2), pl.ds(1 + 2 * other, 2)], x_recv.at[2 * t + other])
         arrived(xe.at[pl.ds(2 * t, 2), pl.ds(5 - 5 * other, 1)], x_recv.at[8 + 2 * t + other])
 
     for a in range(3):
@@ -350,22 +363,24 @@
 
     x_t = xe[2:6, 1:5].reshape(256, 256).astype(F32).T.astype(BF16)
 
-    for t, core in ((2, 0), (2, 1), (1 - s, 0), (1 - s, 1), (s, other)):
-        arrived(te.at[pl.ds(2 * t, 2), pl.ds(1 + 4 * core, 4)], t_recv.at[2 * t + core])
+    for t, core in ((1 - s, c), (2, c), (0, other), (1, other), (2, other)):
+        arrived(tq.at[t, core], t_recv.at[2 * t + core])
     for t in range(3):
-        arrived(te.at[pl.ds(2 * t, 2), pl.ds(9 - 9 * other, 1)], t_recv.at[6 + 2 * t + other])
-
-    def sort_target(f, carry):
-        tf[...] = te[f].astype(F32).reshape(320, 128)
-        for i in range(2):
+        arrived(eq.at[t, other, c], t_recv.at[6 + 2 * t + other])
+
+    for t in range(3):
+        edges = [eq[t, core, c].astype(F32) for core in range(2)]
+        for f in range(2):
             for j in range(2):
-                for r in range(5):
-                    row = 2 * r + 1 - i
-                    v = tf[pl.ds(row * 32 + j, 16, stride=2), :]
-                    tp[f, i, j, r * 16 : (r + 1) * 16, :] = turn(v, -quarter)
-        return carry
-
-    lax.fori_loop(0, 6, sort_target, 0)
+                at = 2 * t + f
+                tp[at, 0, j, 64:80] = turn(edges[0], -(2 * f + j))
+                tp[at, 1, j, 0:16] = turn(edges[1], -(2 * f + j))
+                for core in range(2):
+                    rows = tq[t, core, f, j].astype(F32)
+                    for r in range(2):
+                        for i in range(2):
+                            k = 16 * (2 * core + r + i)
+                            tp[at, i, j, k : k + 16] = turn(rows, -(2 * r + i))
     token_in(1)
     token_out(2)
 
@@ -557,7 +572,7 @@
         copy.wait_send()
     @pl.when(s == 0)
     def _():
-        for copy in target_copies(5, (-1, -2), 2):
+        for copy in late_copies():
             copy.wait_send()
 
     for p in range(BLOCKS):
@@ -619,8 +634,12 @@
             pltpu.VMEM((BLOCKS, 16, 16, 128), BF16),
             pltpu.VMEM((8, 6, 16, 256), BF16),
             pltpu.VMEM((6, 6, 16, 768), BF16),
-            pltpu.VMEM((6, 10, 32, 128), BF16),
-            pltpu.VMEM((320, 128), F32),
+            pltpu.VMEM((2, 4, 32, 128), BF16),
+            pltpu.VMEM((256, 128), F32),
+            pltpu.VMEM((4, 2, 2, 16, 128), BF16),
+            pltpu.VMEM((4, 16, 128), BF16),
+            pltpu.VMEM((3, 2, 2, 2, 16, 128), BF16),
+            pltpu.VMEM((3, 2, 2, 16, 128), BF16),
             pltpu.VMEM((6, 2, 2, 80, 128), F32),
             pltpu.VMEM((6, 96, 384), F32),
             pltpu.VMEM((6, 64, 256), BF16),

time: 63.2 us -> 58.5 us (0.926)
  Pallas kernels: 58.9 us -> 54.2 us
    pallas_call x1, Pallas kernels: 58.9 us -> 54.2 us  [per_device(): pl.pallas_call(kernel, out_shape=(jax.ShapeDtypeStruct(master.shape, F32)...]
where the time goes in v5:
time: 58.5 us; the launch traced here: 58.3 us
  Pallas kernels  54.2 us (93%)
  between operations  2.36 us (4%)
  other arithmetic  1.43 us (2%)
    pallas_call x1, Pallas kernels, per_device(): pl.pallas_call(kernel, out_shape=(jax.ShapeDtypeStruct(master.shape, F32)...  54.2 us

profile of v5, /device:TPU:1, one launch (start us, length us, event | category | flops | bytes accessed | tf_op | source)
XLA Modules:
  0.0 58.3 jit_solution(10481096568770703302)
XLA Ops:
  0.6 0.0 copy-start.2
  0.6 0.0 copy-start.3
  0.7 54.2 %shard_map.109 = (f32[8,3456]{1,0:T(8,128)S(1)}, f32[2,2,16,256]{3,2,1,0:T(8,128)S(1)}, f32[3,2,2,16,256]{4,3,2,1,0:T(8,128)S(1)}, f32[1,1]{1,0:T(1,128)}) custom-call(bf16[2,2,16,256]{3,2,1,0:T(8,128)(2,1)} %latent.1, bf16[2,4,32,128]{3,2,1,0:T(8,128)(2,1)} %target.1, f32[8,3456]{1,0:T(8,128)} %master.1), custom_call_target="tpu_custom_call" | custom-call | tf_op jit(solution)/shard_map/pallas_call | solution.py:620
  54.9 0.0 copy-start
  54.9 0.0 copy-start.1
  54.9 0.6 %fusion.1 = bf16[2,2,16,256]{3,2,1,0:T(8,128)(2,1)} fusion(f32[2,2,16,256]{3,2,1,0:T(8,128)S(1)} %get-tuple-element.11, f32[3,2,2,16,256]{4,3,2,1,0:T(8,128)S(1)} %get-tuple-element.12), kind=kLoop, calls=%fused_computation.6 | loop fusion | flops 65536 | bytes 294912 | tf_op jit(solution)/shard_map/convert_element_type | solution.py:686
  55.5 0.0 copy-done.2
  55.5 0.0 copy-done.3
  55.5 0.2 copy-done
  55.8 0.1 copy-done.1
  55.8 0.8 %multiply_add_fusion = (f32[8,3456]{1,0:T(8,128)}, f32[8,3456]{1,0:T(8,128)}, f32[8,3456]{1,0:T(8,128)}, f32[8,3456]{1,0:T(8,128)}) fusion(f32[8,3456]{1,0:T(8,128)S(1)} %copy-done.1, f32[8,3456]{1,0:T(8,128)S(1)} %copy-done, f32[8,3456]{1,0:T(8,128)S(1)} %get-tuple-element.10, f32[8,3456]{1,0:T(8,128)S(1)} %copy-done.2, f32[8,3456]{1,0:T(8,128)S(1)} %copy-done.3), kind=kLoop, calls=%fused_computation.2 | loop fusion | flops 387072 | bytes 995328 | tf_op jit(solution)/shard_map/add | solution.py:685
Async XLA Ops:
  0.6 54.9 %copy-start.2 = (f32[8,3456]{1,0:T(8,128)S(1)}, f32[8,3456]{1,0:T(8,128)}, u32[]{:S(2)}) copy-start(f32[8,3456]{1,0:T(8,128)} %param.9) | copy-start | bytes 331780
  0.6 54.9 %copy-start.3 = (f32[8,3456]{1,0:T(8,128)S(1)}, f32[8,3456]{1,0:T(8,128)}, u32[]{:S(2)}) copy-start(f32[8,3456]{1,0:T(8,128)} %param.10) | copy-start | bytes 331780
  54.9 0.9 %copy-start = (f32[8,3456]{1,0:T(8,128)S(1)}, f32[8,3456]{1,0:T(8,128)}, u32[]{:S(2)}) copy-start(f32[8,3456]{1,0:T(8,128)} %master.1) | copy-start | bytes 331780
  54.9 1.0 %copy-start.1 = (f32[8,3456]{1,0:T(8,128)S(1)}, f32[8,3456]{1,0:T(8,128)}, u32[]{:S(2)}) copy-start(f32[8,3456]{1,0:T(8,128)} %param.11) | copy-start | bytes 331780

commit v6 on v5

--- a/solution.py
+++ b/solution.py
@@ -18,6 +18,8 @@
 BF16 = jnp.bfloat16
 SCALE = 1.0 / math.sqrt(27 * 256)
 BLOCKS = 7
+OWNERS = 2
+APART = 8 // OWNERS
 Z = 16
 
 
@@ -518,9 +520,16 @@
         kept[i] = jnp.where(c == 0, rows[:, 0:8], rows[:, 8:16])
         send(swap_out.at[part], swap_in.at[part], swap_sem.at[i], swap_sem.at[3 + i], sibling)
 
-    def z_block(p):
+    mine_at = z // 2
+
+    def z_block(p, slot):
+        owner = (p - APART * slot) % 8
         return remote(
-            zsend_buf.at[p], zrecv_buf.at[z // 2], z_send.at[p], z_recv.at[z // 2], (2 * p + s, h)
+            zsend_buf.at[p],
+            zrecv_buf.at[slot, mine_at],
+            z_send.at[OWNERS * p + slot],
+            z_recv.at[8 * slot + mine_at],
+            (2 * owner + s, h),
         )
 
     def along_z(i):
@@ -533,9 +542,11 @@
         ).astype(BF16)
         for p in range(first, first + n):
 
-            @pl.when(z // 2 != p)
-            def _():
-                z_block(p).start()
+            for slot in range(OWNERS):
+
+                @pl.when(mine_at != (p - APART * slot) % 8)
+                def _():
+                    z_block(p, slot).start()
 
     axis_a(0)
     axis_a(1)
@@ -548,23 +559,32 @@
     swap(2)
     along_z(2)
 
-    def g_copy(i):
-        to = (z + i) % Z
-        return remote(gsend_buf, grecv_buf.at[z], g_send.at[i], g_recv.at[z], (to, h))
-
-    order = [8] + [v for d in range(7, 0, -1) for v in (d, 16 - d)]
-
-    @pl.when(z < 14)
-    def _():
-        acc = zsend_buf[z // 2].astype(F32)
-        for i in (1, 7, 2, 6, 3, 5, 4):
-            source = (z // 2 + i) % 8
-            arrived(zrecv_buf.at[source], z_recv.at[source])
-            acc = acc + zrecv_buf[source].astype(F32)
-        gsend_buf[...] = acc.astype(BF16)
-        for i in order:
-            g_copy(i).start()
-        grecv_buf[z] = gsend_buf[...]
+    def g_copy(slot, step):
+        block = 2 * ((mine_at + APART * slot) % 8) + s
+        n = (2 * APART - 1) * slot + (step + APART if step < 0 else step + APART - 1)
+        return remote(
+            gsend_buf.at[slot], grecv_buf.at[block], g_send.at[n], g_recv.at[block], ((z + step + Z) % Z, h)
+        )
+
+    steps = [v for d in range(APART, 0, -1) for v in (-d, d - 1) if v]
+
+    for j in range(OWNERS):
+        slot = (j - mine_at // APART + OWNERS) % OWNERS
+        block = mine_at % APART + APART * j
+
+        @pl.when(block < BLOCKS)
+        def _():
+            zrecv_buf[slot, mine_at] = zsend_buf[block]
+            for i in (1, 7, 2, 6, 3, 5, 4):
+                source = (mine_at + i) % 8
+                arrived(zrecv_buf.at[slot, source], z_recv.at[8 * slot + source])
+            acc = zrecv_buf[slot, 0].astype(F32)
+            for i in range(1, 8):
+                acc = acc + zrecv_buf[slot, i].astype(F32)
+            gsend_buf[slot] = acc.astype(BF16)
+            for step in steps:
+                g_copy(slot, step).start()
+            grecv_buf[2 * block + s] = gsend_buf[slot]
 
     for i in range(3):
         arrived(out_other.at[i], lat_sem.at[3 + i])
@@ -577,9 +597,18 @@
 
     for p in range(BLOCKS):
 
-        @pl.when(z // 2 != p)
+        for slot in range(OWNERS):
+
+            @pl.when(mine_at != (p - APART * slot) % 8)
+            def _():
+                z_block(p, slot).wait_send()
+
+    for slot in range(OWNERS):
+
+        @pl.when((mine_at + APART * slot) % 8 < BLOCKS)
         def _():
-            z_block(p).wait_send()
+            for step in steps:
+                g_copy(slot, step).wait_send()
 
     def grad_tap(t, pieces, group):
         out_grad[:, t * 128 : (t + 1) * 128] = SCALE * by_group(
@@ -591,7 +620,7 @@
         for i in range(2):
             at = 2 * p + i
 
-            @pl.when(z != at)
+            @pl.when((z - at + Z) % (2 * APART) != 0)
             def _():
                 arrived(grecv_buf.at[at], g_recv.at[at])
 
@@ -605,11 +634,6 @@
     whole = (pieces[0] + pieces[1] + pieces[2] + pieces[3])[0:1]
     whole = jnp.where(group_of((1, 128)) == 3, whole, 0.0)
     out_loss[0, 0] = jnp.sum(whole) * (1.0 / 16777216)
-
-    @pl.when(z < 14)
-    def _():
-        for i in order:
-            g_copy(i).wait_send()
 
 
 def per_device(latent, target_frames, master, first_moment, second_moment, ema_weights):
@@ -651,8 +675,8 @@
             pltpu.VMEM((BLOCKS, 8, 128), F32),
             pltpu.VMEM((BLOCKS, 8, 128), F32),
             pltpu.VMEM((BLOCKS, 16, 128), BF16),
-            pltpu.VMEM((8, 16, 128), BF16),
-            pltpu.VMEM((16, 128), BF16),
+            pltpu.VMEM((OWNERS, 8, 16, 128), BF16),
+            pltpu.VMEM((OWNERS, 16, 128), BF16),
             pltpu.VMEM((16, 16, 128), BF16),
             pltpu.VMEM((2, 2, 2, 2, 16, 256), F32),
             dma((2,)),
@@ -667,8 +691,8 @@
             dma((9,)),
             dma((9,)),
             dma((6,)),
-            dma((8,)),
-            dma((8,)),
+            dma((OWNERS * BLOCKS,)),
+            dma((OWNERS * 8,)),
             dma((16,)),
             dma((16,)),
             dma((6,)),

time: 58.5 us -> 56.6 us (0.968)
  Pallas kernels: 54.2 us -> 52.3 us
    pallas_call x1, Pallas kernels: 54.2 us -> 52.3 us  [per_device(): pl.pallas_call(kernel, out_shape=(jax.ShapeDtypeStruct(master.shape, F32)...]
where the time goes in v6:
time: 56.6 us; the launch traced here: 56.4 us
  Pallas kernels  52.3 us (92%)
  between operations  2.36 us (4%)
  other arithmetic  1.43 us (3%)
    pallas_call x1, Pallas kernels, per_device(): pl.pallas_call(kernel, out_shape=(jax.ShapeDtypeStruct(master.shape, F32)...  52.3 us

profile of v6, /device:TPU:1, one launch (start us, length us, event | category | flops | bytes accessed | tf_op | source)
XLA Modules:
  0.0 56.4 jit_solution(13859106884177192586)
XLA Ops:
  0.6 0.0 copy-start.2
  0.6 0.0 copy-start.3
  0.7 52.3 %shard_map.109 = (f32[8,3456]{1,0:T(8,128)S(1)}, f32[2,2,16,256]{3,2,1,0:T(8,128)S(1)}, f32[3,2,2,16,256]{4,3,2,1,0:T(8,128)S(1)}, f32[1,1]{1,0:T(1,128)}) custom-call(bf16[2,2,16,256]{3,2,1,0:T(8,128)(2,1)} %latent.1, bf16[2,4,32,128]{3,2,1,0:T(8,128)(2,1)} %target.1, f32[8,3456]{1,0:T(8,128)} %master.1), custom_call_target="tpu_custom_call" | custom-call | tf_op jit(solution)/shard_map/pallas_call | solution.py:644
  53.0 0.0 copy-start
  53.0 0.0 copy-start.1
  53.0 0.6 %fusion.1 = bf16[2,2,16,256]{3,2,1,0:T(8,128)(2,1)} fusion(f32[2,2,16,256]{3,2,1,0:T(8,128)S(1)} %get-tuple-element.11, f32[3,2,2,16,256]{4,3,2,1,0:T(8,128)S(1)} %get-tuple-element.12), kind=kLoop, calls=%fused_computation.6 | loop fusion | flops 65536 | bytes 294912 | tf_op jit(solution)/shard_map/convert_element_type | solution.py:710
  53.7 0.0 copy-done.2
  53.7 0.0 copy-done.3
  53.7 0.2 copy-done
  53.9 0.1 copy-done.1
  54.0 0.8 %multiply_add_fusion = (f32[8,3456]{1,0:T(8,128)}, f32[8,3456]{1,0:T(8,128)}, f32[8,3456]{1,0:T(8,128)}, f32[8,3456]{1,0:T(8,128)}) fusion(f32[8,3456]{1,0:T(8,128)S(1)} %copy-done.1, f32[8,3456]{1,0:T(8,128)S(1)} %copy-done, f32[8,3456]{1,0:T(8,128)S(1)} %get-tuple-element.10, f32[8,3456]{1,0:T(8,128)S(1)} %copy-done.2, f32[8,3456]{1,0:T(8,128)S(1)} %copy-done.3), kind=kLoop, calls=%fused_computation.2 | loop fusion | flops 387072 | bytes 995328 | tf_op jit(solution)/shard_map/add | solution.py:709
Async XLA Ops:
  0.6 53.0 %copy-start.2 = (f32[8,3456]{1,0:T(8,128)S(1)}, f32[8,3456]{1,0:T(8,128)}, u32[]{:S(2)}) copy-start(f32[8,3456]{1,0:T(8,128)} %param.9) | copy-start | bytes 331780
  0.6 53.0 %copy-start.3 = (f32[8,3456]{1,0:T(8,128)S(1)}, f32[8,3456]{1,0:T(8,128)}, u32[]{:S(2)}) copy-start(f32[8,3456]{1,0:T(8,128)} %param.10) | copy-start | bytes 331780
  53.0 0.9 %copy-start = (f32[8,3456]{1,0:T(8,128)S(1)}, f32[8,3456]{1,0:T(8,128)}, u32[]{:S(2)}) copy-start(f32[8,3456]{1,0:T(8,128)} %master.1) | copy-start | bytes 331780
  53.0 1.0 %copy-start.1 = (f32[8,3456]{1,0:T(8,128)S(1)}, f32[8,3456]{1,0:T(8,128)}, u32[]{:S(2)}) copy-start(f32[8,3456]{1,0:T(8,128)} %param.11) | copy-start | bytes 331780

commit v7 on v6

--- a/solution.py
+++ b/solution.py
@@ -298,6 +298,7 @@
             for copy in late_copies():
                 copy.start()
 
+    send_latent()
     loads[2].wait()
     pack_target()
 
@@ -318,7 +319,6 @@
         send_unit(u, j - 1, unit(j, 0))
     for j in far_first:
         send_unit(u, 2 + j, unit(0, j))
-    send_latent()
     send_target()
     for k in (1, 3, 2):
         index = unit(4 - k, 0)

time: 56.6 us -> 56.8 us (level)
  no operation moved by 1% of the time
where the time goes in v7:
time: 56.8 us; the launch traced here: 56.6 us
  Pallas kernels  52.5 us (92%)
  between operations  2.36 us (4%)
  other arithmetic  1.43 us (3%)
    pallas_call x1, Pallas kernels, per_device(): pl.pallas_call(kernel, out_shape=(jax.ShapeDtypeStruct(master.shape, F32)...  52.5 us

profile of v7, /device:TPU:1, one launch (start us, length us, event | category | flops | bytes accessed | tf_op | source)
XLA Modules:
  0.0 56.6 jit_solution(17198321208442032481)
XLA Ops:
  0.6 0.0 copy-start.2
  0.6 0.0 copy-start.3
  0.7 52.5 %shard_map.109 = (f32[8,3456]{1,0:T(8,128)S(1)}, f32[2,2,16,256]{3,2,1,0:T(8,128)S(1)}, f32[3,2,2,16,256]{4,3,2,1,0:T(8,128)S(1)}, f32[1,1]{1,0:T(1,128)}) custom-call(bf16[2,2,16,256]{3,2,1,0:T(8,128)(2,1)} %latent.1, bf16[2,4,32,128]{3,2,1,0:T(8,128)(2,1)} %target.1, f32[8,3456]{1,0:T(8,128)} %master.1), custom_call_target="tpu_custom_call" | custom-call | tf_op jit(solution)/shard_map/pallas_call | solution.py:644
  53.1 0.0 copy-start
  53.1 0.0 copy-start.1
  53.2 0.6 %fusion.1 = bf16[2,2,16,256]{3,2,1,0:T(8,128)(2,1)} fusion(f32[2,2,16,256]{3,2,1,0:T(8,128)S(1)} %get-tuple-element.11, f32[3,2,2,16,256]{4,3,2,1,0:T(8,128)S(1)} %get-tuple-element.12), kind=kLoop, calls=%fused_computation.6 | loop fusion | flops 65536 | bytes 294912 | tf_op jit(solution)/shard_map/convert_element_type | solution.py:710
  53.8 0.0 copy-done.2
  53.8 0.0 copy-done.3
  53.8 0.2 copy-done
  54.0 0.1 copy-done.1
  54.1 0.8 %multiply_add_fusion = (f32[8,3456]{1,0:T(8,128)}, f32[8,3456]{1,0:T(8,128)}, f32[8,3456]{1,0:T(8,128)}, f32[8,3456]{1,0:T(8,128)}) fusion(f32[8,3456]{1,0:T(8,128)S(1)} %copy-done.1, f32[8,3456]{1,0:T(8,128)S(1)} %copy-done, f32[8,3456]{1,0:T(8,128)S(1)} %get-tuple-element.10, f32[8,3456]{1,0:T(8,128)S(1)} %copy-done.2, f32[8,3456]{1,0:T(8,128)S(1)} %copy-done.3), kind=kLoop, calls=%fused_computation.2 | loop fusion | flops 387072 | bytes 995328 | tf_op jit(solution)/shard_map/add | solution.py:709
Async XLA Ops:
  0.6 53.2 %copy-start.2 = (f32[8,3456]{1,0:T(8,128)S(1)}, f32[8,3456]{1,0:T(8,128)}, u32[]{:S(2)}) copy-start(f32[8,3456]{1,0:T(8,128)} %param.9) | copy-start | bytes 331780
  0.6 53.2 %copy-start.3 = (f32[8,3456]{1,0:T(8,128)S(1)}, f32[8,3456]{1,0:T(8,128)}, u32[]{:S(2)}) copy-start(f32[8,3456]{1,0:T(8,128)} %param.10) | copy-start | bytes 331780
  53.1 0.9 %copy-start = (f32[8,3456]{1,0:T(8,128)S(1)}, f32[8,3456]{1,0:T(8,128)}, u32[]{:S(2)}) copy-start(f32[8,3456]{1,0:T(8,128)} %master.1) | copy-start | bytes 331780
  53.1 1.0 %copy-start.1 = (f32[8,3456]{1,0:T(8,128)S(1)}, f32[8,3456]{1,0:T(8,128)}, u32[]{:S(2)}) copy-start(f32[8,3456]{1,0:T(8,128)} %param.11) | copy-start | bytes 331780
